TPU v7x, 32 devices: a whole 2x2x4 slice. The times are simulated.
32 devices in a mesh: horiz: 8 (over z, y), lev: 4 (over x, core).
Axes of the slice: x: 2, y: 2, z: 4, core: 2. Of those that a mesh axis runs over, the one named last changes fastest.
Arguments:
- control: float32 [64, 32, 4096], P('lev', None, 'horiz'), may hold values from -6 to 6
- members: bfloat16 [64, 4, 32, 4096], P('lev', None, None, 'horiz'), may hold values from -6 to 6
- extinction: float32 [4], replicated, may hold values from 0.5 to 2
- kernels: bfloat16 [4096, 64, 128], P('horiz', 'lev'), may hold values from 0 to 1
- innovation: bfloat16 [4096, 128], P('horiz'), may hold values from -16 to 16
- obs_weight: bfloat16 [4096, 128], P('horiz'), may hold values from 0.25 to 4
- owners: int32 [4096, 1], P('horiz'), may hold values from 0 to 7; in each aligned block of 512 rows (0 to 511, 512 to 1023, ...) at most 128 rows name the same one
- pixel_columns: int32 [4096, 128], P('horiz'), may hold values from 0 to 511
- pixel_counts: int32 [4096], P('horiz'), may hold values from 1 to 128
Outputs:
- gradient: float32 [64, 32, 4096], P('lev', None, 'horiz')
Inputs may be any that keep to these rules, and one draw needn't show every extreme that they name: `owners`: among the 512 blocks of one index of horiz, no owner is named more than 128 times, and in some index's blocks one owner is named exactly 128 times.
All inputs are finite; a program needn't handle non-finite values.
Results may differ from a plain program's by a relative error of at most 0.0037.
Values may be sent and summed in bfloat16 or wider, within the bound.
A program may use at most 128 MiB of HBM per device.

v0:
```python
import functools
import math

import jax
import jax.numpy as jnp
import numpy as np
from jax import lax
from jax.experimental import pallas as pl
from jax.experimental.pallas import tpu as pltpu
from jax.sharding import PartitionSpec as P

LEV = 64
HALF = 4
LANES = 128
PAIR = 16
GROUP = 64
BF = jnp.bfloat16
F32 = jnp.float32


def level_matrix():
    index_levels = np.arange(LEV, dtype=np.float32)
    spread = np.float32(LEV / 8.0)
    distance = index_levels[:, None] - index_levels[None, :]
    matrix = np.exp(-distance * distance / (2 * spread * spread)) / (np.float32(2.5066283) * spread)
    return matrix.astype(BF)


def column_taps():
    offsets = np.arange(2 * HALF + 1, dtype=np.float32) - HALF
    spread = np.float32(HALF / 2.0)
    weights = np.exp(-offsets * offsets / (2 * spread * spread))
    return weights / np.sum(weights)


def tap_matrix(width):
    rows = np.arange(width + LANES)
    place = np.where(rows < width + HALF, rows, rows - width - 2 * HALF)
    gap = place[:, None] - np.arange(width)[None, :]
    near = (np.abs(gap) <= HALF) & (rows < width + 2 * HALF)[:, None]
    dense = np.where(near, column_taps()[np.clip(gap + HALF, 0, 2 * HALF)], 0.0).astype(np.float32)
    high = dense.astype(BF)
    low = (dense - high.astype(np.float32)).astype(BF)
    return jnp.asarray(high), jnp.asarray(low)


def spread_levels(matrix):
    dense = np.kron(matrix.astype(np.float32), np.eye(PAIR, dtype=np.float32))
    return jnp.asarray(dense.astype(BF))


def dot(a, b):
    return jnp.dot(a, b, preferred_element_type=F32)


def field_kernel(scale, all_ref, kron_ref, mixed_ref, out_ref):
    levels, members, width = mixed_ref.shape
    total = None
    for half in range(members // PAIR):
        part = pl.ds(half * PAIR, PAIR)
        x = all_ref[:, part, :].reshape(LEV * PAIR, width)
        inc = dot(kron_ref[...], x).reshape(levels, PAIR, width)
        term = jnp.sum(mixed_ref[:, part, :].astype(F32) * inc, axis=1)
        total = term if total is None else total + term
    total = total * scale
    for tile in range(width // LANES):
        out_ref[tile] = total[:, tile * LANES : (tile + 1) * LANES]


def forward_kernel(owner_ref, field_ref, kern_ref, col_ref, out_ref):
    blocks = col_ref.shape[0]
    tiles, levels = field_ref.shape[1], field_ref.shape[2]

    def step(group, carry):
        base = pl.multiple_of(group * GROUP, GROUP)
        cols = col_ref[pl.ds(base, GROUP), :]
        rows = []
        for i in range(GROUP):
            owner = owner_ref[base + i]
            col = jnp.broadcast_to(cols[i : i + 1, :], (levels, LANES))
            low = jnp.bitwise_and(col, LANES - 1)
            high = jnp.right_shift(col, 7)
            picked = jnp.take_along_axis(field_ref[owner, 0], low, axis=1)
            for tile in range(1, tiles):
                other = jnp.take_along_axis(field_ref[owner, tile], low, axis=1)
                picked = jnp.where(high == tile, other, picked)
            prod = picked * kern_ref[base + i].astype(F32)
            rows.append(jnp.sum(prod, axis=0, keepdims=True))
        out_ref[pl.ds(base, GROUP), :] = jnp.concatenate(rows, axis=0)
        return carry

    lax.fori_loop(0, blocks // GROUP, step, 0)


def adjoint_kernel(scale, owner_ref, kern_ref, col_ref, ev_ref, inn_ref, w_ref, out_ref):
    blocks = col_ref.shape[0]
    levels = kern_ref.shape[1]
    tiles = out_ref.shape[2] // levels
    out_ref[...] = jnp.zeros_like(out_ref)
    lane_row = lax.broadcasted_iota(jnp.int32, (LANES, LANES), 0).astype(F32).astype(BF)
    one, zero = jnp.ones((), BF), jnp.zeros((), BF)

    def step(group, carry):
        base = pl.multiple_of(group * GROUP, GROUP)
        cols = col_ref[pl.ds(base, GROUP), :]
        low = jnp.bitwise_and(cols, LANES - 1).astype(F32)
        high = jnp.right_shift(cols, 7)
        misfit = w_ref[pl.ds(base, GROUP), :] * (
            ev_ref[pl.ds(base, GROUP), :] - inn_ref[pl.ds(base, GROUP), :]
        )
        misfit = misfit * scale
        parts = [jnp.where(high == tile, misfit, 0.0) for tile in range(tiles)]
        for i in range(GROUP):
            owner = owner_ref[base + i]
            kern = kern_ref[base + i].astype(F32)
            rows = jnp.concatenate(
                [(kern * part[i : i + 1, :]).astype(BF) for part in parts], axis=0
            )
            row = jnp.broadcast_to(low[i : i + 1, :], (LANES, LANES)).astype(BF)
            hot = jnp.where(lane_row == row, one, zero)
            out_ref[owner] += lax.dot_general(
                hot, rows, (((1,), (1,)), ((), ())), preferred_element_type=F32
            )
        return carry

    lax.fori_loop(0, blocks // GROUP, step, 0)


def final_kernel(mixed_ref, fg_ref, kron_ref, hi_ref, lo_ref, control_ref, out_ref):
    levels, members, width = control_ref.shape
    ext = mixed_ref.shape[2]
    fg = fg_ref[...]
    for half in range(members // PAIR):
        part = pl.ds(half * PAIR, PAIR)
        grad = mixed_ref[:, part, :].astype(F32) * fg[:, None, :]
        grad = grad.reshape(LEV * PAIR, ext)
        high = grad.astype(BF)
        low = (grad - high.astype(F32)).astype(BF)
        mixed_levels = dot(kron_ref[...], high) + dot(kron_ref[...], low)
        high = mixed_levels.astype(BF)
        low = (mixed_levels - high.astype(F32)).astype(BF)
        total = dot(high, hi_ref[...]) + dot(high, lo_ref[...]) + dot(low, hi_ref[...])
        out_ref[:, part, :] = control_ref[:, part, :] + total.reshape(levels, PAIR, width)


def greet(partners):
    barrier = pltpu.get_barrier_semaphore()
    for device in partners:
        pl.semaphore_signal(barrier, inc=1, device_id=device, device_id_type=MESH)
    pl.semaphore_wait(barrier, len(partners))


def send(src, dst, send_sem, recv_sem, device):
    copy = pltpu.make_async_remote_copy(
        src_ref=src,
        dst_ref=dst,
        send_sem=send_sem,
        recv_sem=recv_sem,
        device_id=device,
        device_id_type=MESH,
    )
    copy.start()
    return copy


def others(axis, count):
    me = lax.axis_index(axis)
    return [lax.rem(me + k, count) for k in range(1, count)]


def prepare_kernel(
    count,
    ext_ref,
    control_ref,
    members_ref,
    hi_ref,
    lo_ref,
    mixed_ref,
    ext_out,
    smooth_ref,
    out_tiles,
    in_tiles,
    send_sem,
    recv_sem,
):
    levels, members, width = control_ref.shape
    me = lax.axis_index("horiz")
    right, left = lax.rem(me + 1, count), lax.rem(me + count - 1, count)
    greet([{"horiz": right}, {"horiz": left}])
    lane = lax.broadcasted_iota(jnp.int32, (levels * members, LANES), 1)

    def mix(tile):
        part = pl.ds(tile * LANES, LANES)
        total = ext_ref[0] * members_ref[:, 0, :, part].astype(F32)
        for species in range(1, members_ref.shape[1]):
            total = total + ext_ref[species] * members_ref[:, species, :, part].astype(F32)
        mixed_ref[:, :, part] = total
        ext_out[:, :, part] = total.astype(BF)
        return total.reshape(levels * members, LANES)

    def own(tile):
        return control_ref[:, :, pl.ds(tile * LANES, LANES)].reshape(levels * members, LANES)

    last = width // LANES - 1
    first_mix, last_mix = mix(0), mix(last)
    to_left = jnp.where(lane < HALF, own(0), pltpu.roll(first_mix, 8, 1))
    to_right = jnp.where(lane < 8, pltpu.roll(own(last), 8, 1), pltpu.roll(last_mix, 16, 1))
    out_tiles[0] = to_left.astype(BF)
    out_tiles[1] = to_right.astype(BF)
    copies = [
        send(out_tiles.at[k], in_tiles.at[k], send_sem.at[k], recv_sem.at[k], {"horiz": peer})
        for k, peer in enumerate((left, right))
    ]
    for tile in range(1, last):
        mix(tile)
    x = control_ref[...].astype(BF).reshape(levels * members, width)
    total = dot(x, hi_ref[pl.ds(0, width), :]) + dot(x, lo_ref[pl.ds(0, width), :])
    for copy in copies:
        copy.wait()
    after = HALF * jnp.where(me < count - 1, 1, 0)
    before = HALF * jnp.where(me > 0, 1, 0)
    bit = jnp.bitwise_and(lane, 7)
    halo = jnp.where(bit < after, in_tiles[0].astype(F32), 0.0)
    halo = jnp.where(
        (bit >= HALF) & (bit < HALF + before), in_tiles[1].astype(F32), halo
    )
    shifted = jnp.where(lane < 8, pltpu.roll(halo, LANES - 8, 1), 0.0)
    ext_out[:, :, pl.ds(width, LANES)] = shifted.astype(BF).reshape(levels, members, LANES)
    halo = jnp.where(lane < 8, halo, 0.0).astype(BF)
    total = total + dot(halo, hi_ref[pl.ds(width, LANES), :])
    total = total + dot(halo, lo_ref[pl.ds(width, LANES), :])
    smooth_ref[...] = total.astype(BF).reshape(levels, members, width)


def gather_kernel(axis, count, x_ref, out_ref, send_sem, recv_sem):
    me = lax.axis_index(axis)
    peers = others(axis, count)
    greet([{axis: peer} for peer in peers])
    copies = [
        send(x_ref, out_ref.at[me], send_sem.at[k], recv_sem.at[k], {axis: peer})
        for k, peer in enumerate(peers)
    ]
    out_ref[me] = x_ref[...]
    for copy in copies:
        copy.wait()


def level_gather_kernel(x_ref, out_ref, far_s, far_r, near_s, near_r, on_s, on_r):
    me = lax.axis_index("lev")
    near = me + 1 - 2 * lax.rem(me, 2)
    far = lax.rem(me + 2, 4)
    greet([{"lev": near}, {"lev": far}])
    chunks = far_s.shape[0]
    rows = x_ref.shape[0] // chunks
    parts = [pl.ds(c * rows, rows) for c in range(chunks)]
    away = [
        send(x_ref.at[part], out_ref.at[me, part], far_s.at[c], far_r.at[c], {"lev": far})
        for c, part in enumerate(parts)
    ]
    beside = send(x_ref, out_ref.at[me], near_s, near_r, {"lev": near})
    out_ref[me] = x_ref[...]
    onward = []
    for c, part in enumerate(parts):
        away[c].wait_recv()
        block = out_ref.at[far, part]
        onward.append(send(block, block, on_s.at[c], on_r.at[c], {"lev": near}))
    for copy in away:
        copy.wait_send()
    beside.wait()
    for copy in onward:
        copy.wait()


def total_kernel(count, x_ref, out_ref, slots, send_a, recv_a, send_b, recv_b):
    me = lax.axis_index("lev")
    peers = others("lev", count)
    greet([{"lev": peer} for peer in peers])
    rows = x_ref.shape[0] // count
    copies = [
        send(
            x_ref.at[pl.ds(pl.multiple_of(peer * rows, rows), rows)],
            slots.at[k],
            send_a.at[k],
            recv_a.at[k],
            {"lev": peer},
        )
        for k, peer in enumerate(peers)
    ]
    mine = pl.ds(pl.multiple_of(me * rows, rows), rows)
    total = x_ref[mine, :]
    for k, copy in enumerate(copies):
        copy.wait()
        total = total + slots[k]
    out_ref[mine, :] = total
    block = out_ref.at[mine]
    copies = [
        send(block, block, send_b.at[k], recv_b.at[k], {"lev": peer})
        for k, peer in enumerate(peers)
    ]
    for copy in copies:
        copy.wait()


def return_kernel(count, levs, x_ref, out_ref, slots, send_a, recv_a, send_b, recv_b):
    me, lev = lax.axis_index("horiz"), lax.axis_index("lev")
    peers = others("horiz", count)
    sides = others("lev", levs)
    greet([{"horiz": peer} for peer in peers] + [{"lev": side} for side in sides])
    copies = [
        send(x_ref.at[peer], slots.at[k], send_a.at[k], recv_a.at[k], {"horiz": peer})
        for k, peer in enumerate(peers)
    ]
    total = x_ref[me]
    for k, copy in enumerate(copies):
        copy.wait()
        total = total + slots[k]
    out_ref[lev] = total
    block = out_ref.at[lev]
    copies = [
        send(block, block, send_b.at[k], recv_b.at[k], {"lev": side})
        for k, side in enumerate(sides)
    ]
    for copy in copies:
        copy.wait()


def vmem(count):
    return [pl.BlockSpec(memory_space=pltpu.VMEM)] * count


def smem(count):
    return [pl.BlockSpec(memory_space=pltpu.SMEM)] * count


MESH = pl.DeviceIdType.MESH
PARAMS = pltpu.CompilerParams(vmem_limit_bytes=48 * 1024 * 1024)


def call(kernel, shape, dtype, scalars, *args):
    return pl.pallas_call(
        kernel,
        out_shape=jax.ShapeDtypeStruct(shape, dtype),
        in_specs=smem(scalars) + vmem(len(args) - scalars),
        out_specs=pl.BlockSpec(memory_space=pltpu.VMEM),
        compiler_params=PARAMS,
    )(*args)


def exchange(kernel, number, shape, slots, sems, x):
    scratch = [pltpu.VMEM(slots, F32)] if slots else []
    scratch += [pltpu.SemaphoreType.DMA(size) for size in sems]
    return pl.pallas_call(
        kernel,
        out_shape=jax.ShapeDtypeStruct(shape, x.dtype),
        in_specs=vmem(1),
        out_specs=pl.BlockSpec(memory_space=pltpu.VMEM),
        scratch_shapes=scratch,
        compiler_params=pltpu.CompilerParams(
            vmem_limit_bytes=32 * 1024 * 1024, collective_id=number, has_side_effects=True
        ),
    )(x)


def body(
    control,
    members,
    extinction,
    kernels,
    innovation,
    obs_weight,
    owners,
    pixel_columns,
    pixel_counts,
):
    levels, mem_count, width = control.shape
    blocks, _, pixels = kernels.shape
    horiz = lax.axis_size("horiz")
    tiles = width // LANES
    level_loc = level_matrix()
    first = lax.axis_index("lev") * levels
    kron = lax.dynamic_slice_in_dim(
        spread_levels(level_loc), first * PAIR, levels * PAIR, 0
    )
    levs = lax.axis_size("lev")
    hi, lo = tap_matrix(width)
    scale = 1.0 / math.sqrt(mem_count)
    owner_ids = owners[:, 0]

    strip = (levels, mem_count, width)
    edge_tiles = pltpu.VMEM((2, levels * mem_count, LANES), BF)
    mixed, mixed_ext, smooth = pl.pallas_call(
        functools.partial(prepare_kernel, horiz),
        out_shape=[
            jax.ShapeDtypeStruct(strip, F32),
            jax.ShapeDtypeStruct((levels, mem_count, width + LANES), BF),
            jax.ShapeDtypeStruct(strip, BF),
        ],
        in_specs=smem(1) + vmem(4),
        out_specs=vmem(3),
        scratch_shapes=[edge_tiles, edge_tiles] + [pltpu.SemaphoreType.DMA((2,))] * 2,
        compiler_params=pltpu.CompilerParams(
            vmem_limit_bytes=40 * 1024 * 1024, collective_id=4, has_side_effects=True
        ),
    )(extinction, control, members, hi, lo)
    smooth_all = exchange(
        level_gather_kernel,
        0,
        (levs,) + smooth.shape,
        None,
        [(8,), (8,), (), (), (8,), (8,)],
        smooth,
    ).reshape((levs * levels,) + smooth.shape[1:])

    smooth_all, mixed_ext = lax.optimization_barrier((smooth_all, mixed_ext))
    mixed_all = lax.all_gather(mixed_ext, "lev", axis=0, tiled=True)

    field = call(
        functools.partial(field_kernel, scale),
        (tiles, levels, LANES),
        F32,
        0,
        smooth_all,
        kron,
        mixed,
    )
    field_all = exchange(
        functools.partial(gather_kernel, "horiz", horiz),
        1,
        (horiz,) + field.shape,
        None,
        [(horiz - 1,)] * 2,
        field,
    )
    local = call(
        forward_kernel, (blocks, pixels), F32, 1, owner_ids, field_all, kernels, pixel_columns
    )
    evolved = exchange(
        functools.partial(total_kernel, levs),
        2,
        local.shape,
        (levs - 1, blocks // levs, pixels),
        [(levs - 1,)] * 4,
        local,
    )
    live = jnp.arange(pixels, dtype=jnp.int32)[None, :] < pixel_counts[:, None]
    weight = jnp.where(live, obs_weight.astype(F32), 0.0)
    partial = call(
        functools.partial(adjoint_kernel, scale),
        (horiz, LANES, tiles * levels),
        F32,
        1,
        owner_ids,
        kernels,
        pixel_columns,
        evolved,
        innovation.astype(F32),
        weight,
    )
    partial = partial.reshape(horiz, LANES, tiles, levels).transpose(0, 3, 2, 1)
    partial = partial.reshape(horiz, levels, width)
    edge = jnp.zeros((1, levels, HALF), F32)
    after = jnp.concatenate([partial[1:, :, :HALF], edge], axis=0)
    before = jnp.concatenate([edge, partial[:-1, :, width - HALF :]], axis=0)
    blank = jnp.zeros((horiz, levels, LANES - 2 * HALF), F32)
    partial = jnp.concatenate([partial, after, before, blank], axis=2)
    fg_all = exchange(
        functools.partial(return_kernel, horiz, levs),
        3,
        (levs, levels, width + LANES),
        (horiz - 1, levels, width + LANES),
        [(horiz - 1,)] * 2 + [(levs - 1,)] * 2,
        partial,
    ).reshape(levs * levels, width + LANES)
    return call(
        final_kernel, control.shape, F32, 0, mixed_all, fg_all, kron, hi, lo, control
    )


def solution(mesh):
    placed = (
        P("lev", None, "horiz"),
        P("lev", None, None, "horiz"),
        P(),
        P("horiz", "lev", None),
        P("horiz", None),
        P("horiz", None),
        P("horiz", None),
        P("horiz", None),
        P("horiz"),
    )
    return jax.shard_map(
        body, mesh=mesh, in_specs=placed, out_specs=P("lev", None, "horiz"), check_vma=False
    )
```

profile of v0, /device:TPU:0, one launch (start us, length us, event | category | flops | bytes accessed | tf_op | source)
XLA Modules:
  0.0 106.8 jit_solution(14465888024073126152)
XLA Ops:
  6.5 0.0 all-gather.2.cloned.1.call-start
  6.5 0.0 copy-start.1
  6.5 1.2 %copy-done.1 = f32[16,32,512]{2,1,0:T(8,128)S(1)} copy-done((f32[16,32,512]{2,1,0:T(8,128)S(1)}, f32[16,32,512]{2,1,0:T(8,128)}, u32[]{:S(2)}) %copy-start.1) | copy-done | bytes 1048600
  7.8 0.0 copy-start.4
  7.8 1.1 %copy-done.4 = bf16[640,512]{1,0:T(8,128)(2,1)S(1)} copy-done((bf16[640,512]{1,0:T(8,128)(2,1)S(1)}, bf16[640,512]{1,0:T(8,128)(2,1)}, u32[]{:S(2)}) %copy-start.4) | copy-done | bytes 655384
  8.9 0.0 copy-start.6
  8.9 1.1 %copy-done.6 = bf16[640,512]{1,0:T(8,128)(2,1)S(1)} copy-done((bf16[640,512]{1,0:T(8,128)(2,1)S(1)}, bf16[640,512]{1,0:T(8,128)(2,1)}, u32[]{:S(2)}) %copy-start.6) | copy-done | bytes 655384
  9.9 0.0 copy-start.8
  9.9 1.6 %copy-done.8 = bf16[16,4,32,512]{3,2,1,0:T(8,128)(2,1)S(1)} copy-done((bf16[16,4,32,512]{3,2,1,0:T(8,128)(2,1)S(1)}, bf16[16,4,32,512]{3,2,1,0:T(8,128)(2,1)}, u32[]{:S(2)}) %copy-start.8) | copy-done | bytes 2097176
  11.5 0.0 copy-start.13
  11.5 0.7 copy-done.13
  12.2 12.7 %shard_map.118 = (f32[16,32,512]{2,1,0:T(8,128)S(1)}, bf16[16,32,640]{2,1,0:T(8,128)(2,1)}, bf16[16,32,512]{2,1,0:T(8,128)(2,1)S(1)}) custom-call(f32[4]{0:T(128)S(1)} %copy-done.13, f32[16,32,512]{2,1,0:T(8,128)S(1)} %copy-done.1, bf16[16,4,32,512]{3,2,1,0:T(8,128)(2,1)S(1)} %copy-done.8, bf16[640,512]{1,0:T(8,128)(2,1)S(1)} %copy-done.4, ...), custom_call_target="tpu_custom_call" | custom-call | tf_op jit(solution)/shard_map/pallas_call | solution.py:391
  24.8 0.0 copy-start.9
  24.9 1.0 copy-done.9
  25.8 15.3 %shard_map.119 = bf16[4,16,32,512]{3,2,1,0:T(8,128)(2,1)S(1)} custom-call(bf16[16,32,512]{2,1,0:T(8,128)(2,1)S(1)} %get-tuple-element.10.x_ref), custom_call_target="tpu_custom_call" | custom-call | tf_op jit(solution)/shard_map/pallas_call | solution.py:352
  41.1 0.0 all-gather.2.cloned.1.call-update
  41.1 1.1 %constant_dynamic-slice_fusion.kron_ref = bf16[256,1024]{1,0:T(8,128)(2,1)S(1)} fusion(bf16[1024,1024]{1,0:T(8,128)(2,1)} %constant.7.clone, s32[]{:T(128)S(6)} %select_n.7), kind=kLoop, calls=%fused_computation.12 | loop fusion | bytes 1048580 | tf_op jit(solution)/shard_map/dynamic_slice | solution.py:381
  42.2 0.0 copy-start
  42.2 0.0 copy-start.10
  42.3 1.4 %copy-done.10 = f32[16,32,512]{2,1,0:T(8,128)S(1)} copy-done((f32[16,32,512]{2,1,0:T(8,128)S(1)}, f32[16,32,512]{2,1,0:T(8,128)}, u32[]{:S(2)}) %copy-start.10) | copy-done | bytes 1048600
  43.6 0.0 copy-start.11
  43.6 0.0 copy-start.12
  43.6 0.8 shard_map.120.x_ref
  44.4 0.0 copy-start.14
  44.4 0.0 copy-start.15
  44.4 0.0 copy-start.16
  44.4 9.3 %shard_map.121.field_ref = f32[8,4,16,128]{3,2,1,0:T(8,128)S(1)} custom-call(f32[4,16,128]{2,1,0:T(8,128)S(1)} %shard_map.120.x_ref), custom_call_target="tpu_custom_call" | custom-call | tf_op jit(solution)/shard_map/pallas_call | solution.py:352
  53.7 0.0 copy-done
  53.7 0.0 copy-done.11
  53.8 0.0 copy-done.12
  53.8 7.3 %shard_map.122.x_ref = f32[512,128]{1,0:T(8,128)S(1)} custom-call(s32[512]{0:T(512)S(1)} %bitcast.12, f32[8,4,16,128]{3,2,1,0:T(8,128)S(1)} %shard_map.121.field_ref, bf16[512,16,128]{2,1,0:T(8,128)(2,1)S(1)} %copy-done, s32[512,128]{1,0:T(8,128)S(1)} %copy-done.11), custom_call_target="tpu_custom_call" | custom-call | tf_op jit(solution)/shard_map/pallas_call | solution.py:340
  61.1 9.0 %shard_map.123.ev_ref = f32[512,128]{1,0:T(8,128)S(1)} custom-call(f32[512,128]{1,0:T(8,128)S(1)} %shard_map.122.x_ref), custom_call_target="tpu_custom_call" | custom-call | tf_op jit(solution)/shard_map/pallas_call | solution.py:352
  70.1 0.0 copy-done.14
  70.1 0.0 copy-done.15
  70.1 0.0 copy-done.16
  70.1 0.1 convert_select_fusion.w_ref
  70.3 6.6 %shard_map.124 = f32[8,128,64]{2,1,0:T(8,128)S(1)} custom-call(s32[512]{0:T(512)S(1)} %bitcast.13, bf16[512,16,128]{2,1,0:T(8,128)(2,1)S(1)} %copy-done, s32[512,128]{1,0:T(8,128)S(1)} %copy-done.11, f32[512,128]{1,0:T(8,128)S(1)} %shard_map.123.ev_ref, f32[512,128]{1,0:T(8,128)S(1)} %convert_element_type.6.inn_ref, f32[512,128]{1,0:T(8,128)S(1)} %convert_select_fusion.w_ref), custom_call_target="tpu_custom_call" | custom-call | tf_op jit(solution)/shard_map/pallas_call | solution.py:340
  76.8 0.0 copy-start.2
  76.8 0.0 copy-start.5
  76.9 0.0 copy-start.7
  76.9 0.9 copy.16
  77.8 1.0 copy.20
  78.7 0.1 pad.5.clone
  78.8 0.1 fusion.3
  78.9 0.1 fusion.x_ref
  79.0 14.8 %shard_map.125 = f32[4,16,640]{2,1,0:T(8,128)S(1)} custom-call(f32[8,16,640]{2,1,0:T(8,128)S(1)} %fusion.x_ref), custom_call_target="tpu_custom_call" | custom-call | tf_op jit(solution)/shard_map/pallas_call | solution.py:352
  93.8 0.0 all-gather.2.cloned.1.call-done.mixed_ref
  93.8 0.0 copy-done.2
  93.9 0.0 copy-done.5
  93.9 0.0 copy-done.7
  93.9 0.0 copy-start.3
  93.9 1.7 %copy-done.3 = bf16[64,32,640]{2,1,0:T(8,128)(2,1)S(1)} copy-done((bf16[64,32,640]{2,1,0:T(8,128)(2,1)S(1)}, bf16[64,32,640]{2,1,0:T(8,128)(2,1)}, u32[]{:S(2)}) %copy-start.3) | copy-done | bytes 2621464
  95.6 4.3 %shard_map.126 = f32[16,32,512]{2,1,0:T(8,128)} custom-call(bf16[64,32,640]{2,1,0:T(8,128)(2,1)S(1)} %copy-done.3, f32[64,640]{1,0:T(8,128)S(1)} %bitcast.11, bf16[256,1024]{1,0:T(8,128)(2,1)S(1)} %constant_dynamic-slice_fusion.kron_ref, bf16[640,512]{1,0:T(8,128)(2,1)S(1)} %copy-done.5, bf16[640,512]{1,0:T(8,128)(2,1)S(1)} %copy-done.7, ...), custom_call_target="tpu_custom_call" | custom-call | tf_op jit(solution)/shard_map/pallas_call | solution.py:340
  (2 shorter events, 0.0 us)
Async XLA Ops:
  6.5 87.3 %all-gather.2.cloned.1.call-start = ((), (), s32[]{:S(2)}) async-start(), calls=%async_computation | async-start | bytes 3276800 | tf_op jit(solution)/shard_map/all_gather | solution.py:415
  6.5 1.2 %copy-start.1 = (f32[16,32,512]{2,1,0:T(8,128)S(1)}, f32[16,32,512]{2,1,0:T(8,128)}, u32[]{:S(2)}) copy-start(f32[16,32,512]{2,1,0:T(8,128)} %control_ref.3) | copy-start | bytes 3145732
  7.8 1.1 %copy-start.4 = (bf16[640,512]{1,0:T(8,128)(2,1)S(1)}, bf16[640,512]{1,0:T(8,128)(2,1)}, u32[]{:S(2)}) copy-start(bf16[640,512]{1,0:T(8,128)(2,1)} %constant.22.clone.hi_ref) | copy-start | bytes 1966084
  8.9 1.1 %copy-start.6 = (bf16[640,512]{1,0:T(8,128)(2,1)S(1)}, bf16[640,512]{1,0:T(8,128)(2,1)}, u32[]{:S(2)}) copy-start(bf16[640,512]{1,0:T(8,128)(2,1)} %constant.23.clone.lo_ref) | copy-start | bytes 1966084
  9.9 1.6 %copy-start.8 = (bf16[16,4,32,512]{3,2,1,0:T(8,128)(2,1)S(1)}, bf16[16,4,32,512]{3,2,1,0:T(8,128)(2,1)}, u32[]{:S(2)}) copy-start(bf16[16,4,32,512]{3,2,1,0:T(8,128)(2,1)} %members_ref.1) | copy-start | bytes 6291460
  11.5 0.7 copy-start.13
  24.8 1.0 copy-start.9
  42.2 11.5 %copy-start = (bf16[512,16,128]{2,1,0:T(8,128)(2,1)S(1)}, bf16[512,16,128]{2,1,0:T(8,128)(2,1)}, u32[]{:S(2)}) copy-start(bf16[512,16,128]{2,1,0:T(8,128)(2,1)} %kern_ref.3) | copy-start | bytes 6291460
  42.2 1.4 %copy-start.10 = (f32[16,32,512]{2,1,0:T(8,128)S(1)}, f32[16,32,512]{2,1,0:T(8,128)}, u32[]{:S(2)}) copy-start(f32[16,32,512]{2,1,0:T(8,128)} %copy-done.9) | copy-start | bytes 3145732
  43.6 10.1 %copy-start.11 = (s32[512,128]{1,0:T(8,128)S(1)}, s32[512,128]{1,0:T(8,128)}, u32[]{:S(2)}) copy-start(s32[512,128]{1,0:T(8,128)} %col_ref.3) | copy-start | bytes 786436
  43.6 10.1 %copy-start.12 = (s32[512,1]{0,1:T(1,128)S(1)}, s32[512,1]{0,1:T(1,128)}, u32[]{:S(2)}) copy-start(s32[512,1]{0,1:T(1,128)} %param.18) | copy-start | bytes 6148
  44.4 25.7 %copy-start.14 = (bf16[512,128]{1,0:T(8,128)(2,1)S(1)}, bf16[512,128]{1,0:T(8,128)(2,1)}, u32[]{:S(2)}) copy-start(bf16[512,128]{1,0:T(8,128)(2,1)} %param.16) | copy-start | bytes 393220
  44.4 25.7 %copy-start.15 = (bf16[512,128]{1,0:T(8,128)(2,1)S(1)}, bf16[512,128]{1,0:T(8,128)(2,1)}, u32[]{:S(2)}) copy-start(bf16[512,128]{1,0:T(8,128)(2,1)} %param.17) | copy-start | bytes 393220
  44.4 25.7 %copy-start.16 = (s32[512]{0:T(512)S(1)}, s32[512]{0:T(512)}, u32[]{:S(2)}) copy-start(s32[512]{0:T(512)} %param.20) | copy-start | bytes 6148
  76.8 17.0 %copy-start.2 = (f32[16,32,512]{2,1,0:T(8,128)S(1)}, f32[16,32,512]{2,1,0:T(8,128)}, u32[]{:S(2)}) copy-start(f32[16,32,512]{2,1,0:T(8,128)} %control_ref.3) | copy-start | bytes 3145732
  76.8 17.0 %copy-start.5 = (bf16[640,512]{1,0:T(8,128)(2,1)S(1)}, bf16[640,512]{1,0:T(8,128)(2,1)}, u32[]{:S(2)}) copy-start(bf16[640,512]{1,0:T(8,128)(2,1)} %constant.22.clone.hi_ref) | copy-start | bytes 1966084
  76.9 17.0 %copy-start.7 = (bf16[640,512]{1,0:T(8,128)(2,1)S(1)}, bf16[640,512]{1,0:T(8,128)(2,1)}, u32[]{:S(2)}) copy-start(bf16[640,512]{1,0:T(8,128)(2,1)} %constant.23.clone.lo_ref) | copy-start | bytes 1966084
  93.9 1.7 %copy-start.3 = (bf16[64,32,640]{2,1,0:T(8,128)(2,1)S(1)}, bf16[64,32,640]{2,1,0:T(8,128)(2,1)}, u32[]{:S(2)}) copy-start(bf16[64,32,640]{2,1,0:T(8,128)(2,1)} %all-gather.2.cloned.1.call-done.mixed_ref) | copy-start | bytes 7864324
Sparse Core Ops, SparseCore 0:
  41.3 25.4 all-gather.1
where the time goes:
time: 108 us; the launch traced here: 107 us
  Pallas kernels  80 us (74%)
  between operations  13.7 us (13%)
  local copies, waits for them, and re-layouts  12.9 us (12%)
    pallas_call x4, Pallas kernels, exchange(): pl.pallas_call(kernel, out_shape=jax.ShapeDtypeStruct(shape, x.dtype), in...  48.4 us
    pallas_call x4, Pallas kernels, call(): pl.pallas_call(kernel, out_shape=jax.ShapeDtypeStruct(shape, dtype), in_s...  19 us
    pallas_call x1, Pallas kernels, body(): pl.pallas_call(functools.partial(prepare_kernel, horiz), out_shape=[jax.S...  12.7 us
    unnamed x34, local copies, waits for them, and re-layouts  9.76 us
  transfers between devices with their start and end apart: 1, of which 0 were waited for; matrix products, arithmetic and copies ran while one was open for 3% of the time, Pallas kernels for 45%

commit v1 on v0

v1 whole, which is shorter than its diff:
```python
import functools
import math

import jax
import jax.numpy as jnp
import numpy as np
from jax import lax
from jax.experimental import pallas as pl
from jax.experimental.pallas import tpu as pltpu
from jax.sharding import PartitionSpec as P

LEV = 64
HALF = 4
LANES = 128
PAIR = 16
GROUP = 64
BF = jnp.bfloat16
F32 = jnp.float32
MESH = pl.DeviceIdType.MESH
MIB = 1024 * 1024


def level_matrix():
    index_levels = np.arange(LEV, dtype=np.float32)
    spread = np.float32(LEV / 8.0)
    distance = index_levels[:, None] - index_levels[None, :]
    matrix = np.exp(-distance * distance / (2 * spread * spread)) / (np.float32(2.5066283) * spread)
    return matrix.astype(BF)


def column_taps():
    offsets = np.arange(2 * HALF + 1, dtype=np.float32) - HALF
    spread = np.float32(HALF / 2.0)
    weights = np.exp(-offsets * offsets / (2 * spread * spread))
    return weights / np.sum(weights)


def tap_matrix(width):
    rows = np.arange(width + LANES)
    place = np.where(rows < width + HALF, rows, rows - width - LANES)
    used = (rows < width + HALF) | (rows >= width + LANES - HALF)
    gap = place[:, None] - np.arange(width)[None, :]
    near = (np.abs(gap) <= HALF) & used[:, None]
    dense = np.where(near, column_taps()[np.clip(gap + HALF, 0, 2 * HALF)], 0.0).astype(np.float32)
    high = dense.astype(BF)
    low = (dense - high.astype(np.float32)).astype(BF)
    return high, low


def spread_levels(matrix):
    dense = np.kron(matrix.astype(np.float32), np.eye(PAIR, dtype=np.float32))
    return jnp.asarray(dense.astype(BF))


def dot(a, b):
    return jnp.dot(a, b, preferred_element_type=F32)


def greet(partners):
    barrier = pltpu.get_barrier_semaphore()
    for device in partners:
        pl.semaphore_signal(barrier, inc=1, device_id=device, device_id_type=MESH)
    pl.semaphore_wait(barrier, len(partners))


def remote(src, dst, send_sem, recv_sem, device):
    return pltpu.make_async_remote_copy(
        src_ref=src,
        dst_ref=dst,
        send_sem=send_sem,
        recv_sem=recv_sem,
        device_id=device,
        device_id_type=MESH,
    )


def send(*args):
    copy = remote(*args)
    copy.start()
    return copy


def fetch(src, dst, sem):
    copy = pltpu.make_async_copy(src, dst, sem)
    copy.start()
    return copy


def others(axis, count):
    me = lax.axis_index(axis)
    return [lax.rem(me + k, count) for k in range(1, count)]


def flip(index):
    return index + 1 - 2 * lax.rem(index, 2)


def front_kernel(
    levs,
    count,
    scale,
    ext_hbm,
    owner_hbm,
    control_hbm,
    members_hbm,
    kern_hbm,
    col_hbm,
    inn_hbm,
    w_hbm,
    cnt_hbm,
    kron_hbm,
    hi_hbm,
    lo_hbm,
    misfit_ref,
    mixed_all,
    ext_s,
    owner_s,
    control_v,
    members_v,
    kern_v,
    col_v,
    inn_v,
    w_v,
    cnt_v,
    kron_v,
    hi_v,
    lo_v,
    ctrl_all,
    mixed_v,
    halo_v,
    vert_v,
    field_all,
    field_v,
    part_v,
    slots,
    local_sem,
    ctl_sem,
    c_far,
    c_near,
    c_on,
    h_sem,
    z_sem,
    y_sem,
    t_sem,
    g_sem,
    m_far,
    m_near,
    m_on,
):
    levels, members, width = control_v.shape
    tiles = width // LANES
    halves = members // PAIR
    blocks = col_v.shape[0]
    rows = blocks // levs
    lev, me = lax.axis_index("lev"), lax.axis_index("horiz")
    near, far = flip(lev), lax.rem(lev + 2, levs)
    across = flip(far)
    right, left = lax.rem(me + 1, count), lax.rem(me + count - 1, count)
    own = pl.ds(pl.multiple_of(lev * levels, levels), levels)
    afar = pl.ds(pl.multiple_of(far * levels, levels), levels)
    mine = pl.ds(pl.multiple_of(lev * rows, rows), rows)

    tile_cols = [pl.ds(t * LANES, LANES) for t in range(tiles)]
    ctl = [
        fetch(control_hbm.at[:, :, c], control_v.at[:, :, c], ctl_sem.at[t])
        for t, c in enumerate(tile_cols)
    ]
    local = [
        fetch(src, dst, local_sem.at[k])
        for k, (src, dst) in enumerate(
            [
                (ext_hbm, ext_s),
                (members_hbm, members_v),
                (
                    kron_hbm.at[pl.ds(pl.multiple_of(lev * levels * PAIR, levels * PAIR), levels * PAIR)],
                    kron_v,
                ),
                (hi_hbm, hi_v),
                (lo_hbm, lo_v),
                (owner_hbm, owner_s),
                (kern_hbm, kern_v),
                (col_hbm, col_v),
                (inn_hbm.at[mine], inn_v),
                (w_hbm.at[mine], w_v),
                (cnt_hbm, cnt_v),
            ]
        )
    ]
    greet(
        [{"lev": side} for side in others("lev", levs)]
        + [{"horiz": peer} for peer in others("horiz", count)]
    )

    away, beside = [], []
    for t, c in enumerate(tile_cols):
        ctl[t].wait()
        for half in range(halves):
            ctrl_all[half, own, :, c] = control_v[:, pl.ds(half * PAIR, PAIR), c].astype(BF)
        block = ctrl_all.at[:, own, :, c]
        away.append(send(block, block, c_far.at[0, t], c_far.at[1, t], {"lev": far}))
        beside.append(send(block, block, c_near.at[0, t], c_near.at[1, t], {"lev": near}))

    local[0].wait()
    local[1].wait()

    def mix(t):
        total = ext_s[0] * members_v[:, 0, :, tile_cols[t]].astype(F32)
        for species in range(1, members_v.shape[1]):
            total = total + ext_s[species] * members_v[:, species, :, tile_cols[t]].astype(F32)
        mixed_v[:, :, tile_cols[t]] = total
        for half in range(halves):
            mixed_all[half, own, :, tile_cols[t]] = total[:, half * PAIR : (half + 1) * PAIR].astype(BF)

    mix(0)
    mix(tiles - 1)
    edges = [
        send(
            mixed_all.at[:, own, :, tile_cols[t]],
            halo_v.at[k],
            h_sem.at[0, k],
            h_sem.at[1, k],
            {"horiz": peer},
        )
        for k, (t, peer) in enumerate(((0, left), (tiles - 1, right)))
    ]
    for t in range(1, tiles - 1):
        mix(t)

    onward = []

    def pass_on(t):
        away[t].wait_recv()
        block = ctrl_all.at[:, afar, :, tile_cols[t]]
        onward.append(send(block, block, c_on.at[0, t], c_on.at[1, t], {"lev": near}))

    pass_on(0)
    for edge in edges:
        edge.wait()
    lane = lax.broadcasted_iota(jnp.int32, (1, 1, LANES), 2)
    after = HALF * jnp.where(me < count - 1, 1, 0)
    before = LANES - HALF * jnp.where(me > 0, 1, 0)
    for half in range(halves):
        halo = jnp.where(lane < after, halo_v[0, half].astype(F32), 0.0)
        halo = jnp.where(lane >= before, halo_v[1, half].astype(F32), halo)
        mixed_v[:, pl.ds(half * PAIR, PAIR), pl.ds(width, LANES)] = halo
        mixed_all[half, own, :, pl.ds(width, LANES)] = halo.astype(BF)

    local[2].wait()
    for t, c in enumerate(tile_cols):
        if t:
            pass_on(t)
        beside[t].wait_recv()
        onward[t].wait_recv()
        for half in range(halves):
            x = ctrl_all[half, :, :, c].reshape(LEV * PAIR, LANES)
            vert_v[half, :, c] = dot(kron_v[...], x).astype(BF)

    local[3].wait()
    local[4].wait()
    total = None
    for half in range(halves):
        v = vert_v[half]
        inc = dot(v, hi_v[...]) + dot(v, lo_v[...])
        inc = inc.reshape(levels, PAIR, width + LANES)
        term = jnp.sum(mixed_v[:, pl.ds(half * PAIR, PAIR), :] * inc, axis=1)
        total = term if total is None else total + term
    total = total * scale
    for t in range(tiles + 1):
        field_all[me, t] = total[:, t * LANES : (t + 1) * LANES].astype(BF)

    beyond = [lax.rem(me + 2 * k, count) for k in range(1, count // 2)]
    beyond_from = [lax.rem(me + count - 2 * k, count) for k in range(1, count // 2)]
    pair = flip(me)
    block = field_all.at[me]
    z_copies = [
        send(block, block, z_sem.at[0, k], z_sem.at[1, k], {"horiz": peer})
        for k, peer in enumerate(beyond)
    ]
    y_copies = [send(block, block, y_sem.at[0, 0], y_sem.at[1, 0], {"horiz": pair})]
    for k, peer in enumerate(beyond_from):
        z_copies[k].wait_recv()
        block = field_all.at[peer]
        y_copies.append(send(block, block, y_sem.at[0, k + 1], y_sem.at[1, k + 1], {"horiz": pair}))

    m_away, m_beside, m_onward = [], [], []
    for half in range(halves):
        block = mixed_all.at[half, own]
        m_away.append(send(block, block, m_far.at[0, half], m_far.at[1, half], {"lev": far}))
        m_beside.append(send(block, block, m_near.at[0, half], m_near.at[1, half], {"lev": near}))

    for copy in y_copies:
        copy.wait_recv()
    lane2 = lax.broadcasted_iota(jnp.int32, (levels, LANES), 1)
    for h in range(count):
        for t in range(tiles):
            value = field_all[h, t].astype(F32)
            if t == 0 and h > 0:
                value = value + jnp.where(lane2 < HALF, field_all[h - 1, tiles].astype(F32), 0.0)
            if t == tiles - 1 and h < count - 1:
                value = value + jnp.where(
                    lane2 >= LANES - HALF, field_all[h + 1, tiles].astype(F32), 0.0
                )
            field_v[h, t] = value

    for k in range(5, 8):
        local[k].wait()

    def one_peer(k, carry):
        peer = jnp.where(k == 0, far, jnp.where(k == 1, across, jnp.where(k == 2, near, lev)))
        start = pl.multiple_of(peer * rows, rows)

        def step(group, carry):
            base = pl.multiple_of(start + group * GROUP, GROUP)
            cols = col_v[pl.ds(base, GROUP), :]
            out = []
            for i in range(GROUP):
                owner = owner_s[base + i]
                col = jnp.broadcast_to(cols[i : i + 1, :], (levels, LANES))
                low = jnp.bitwise_and(col, LANES - 1)
                high = jnp.right_shift(col, 7)
                picked = jnp.take_along_axis(field_v[owner, 0], low, axis=1)
                for tile in range(1, tiles):
                    other = jnp.take_along_axis(field_v[owner, tile], low, axis=1)
                    picked = jnp.where(high == tile, other, picked)
                prod = picked * kern_v[base + i].astype(F32)
                out.append(jnp.sum(prod, axis=0, keepdims=True))
            part_v[pl.ds(base, GROUP), :] = jnp.concatenate(out, axis=0)
            return carry

        lax.fori_loop(0, rows // GROUP, step, 0)

        @pl.when(k < levs - 1)
        def _():
            remote(
                part_v.at[pl.ds(start, rows)], slots.at[k], t_sem.at[0, k], t_sem.at[1, k], {"lev": peer}
            ).start()

        return carry

    lax.fori_loop(0, levs, one_peer, 0)

    for half in range(halves):
        m_away[half].wait_recv()
        block = mixed_all.at[half, afar]
        m_onward.append(send(block, block, m_on.at[0, half], m_on.at[1, half], {"lev": near}))

    for k in range(8, 11):
        local[k].wait()
    counts = jnp.transpose(jnp.broadcast_to(cnt_v[pl.ds(lev, 1), :].astype(F32), (LANES, LANES)))
    live = lax.broadcasted_iota(jnp.int32, (rows, LANES), 1).astype(F32) < counts
    total = part_v[mine, :]
    sides = [far, across, near]
    for k, side in enumerate(sides):
        start = pl.multiple_of(side * rows, rows)
        copy = remote(
            part_v.at[pl.ds(start, rows)], slots.at[k], t_sem.at[0, k], t_sem.at[1, k], {"lev": side}
        )
        copy.wait()
        total = total + slots[k]
    misfit = w_v[...].astype(F32) * (total - inn_v[...].astype(F32)) * scale
    misfit_ref[mine, :] = jnp.where(live, misfit, 0.0).astype(BF)
    block = misfit_ref.at[mine]
    spread = [
        send(block, block, g_sem.at[0, k], g_sem.at[1, k], {"lev": side})
        for k, side in enumerate(sides)
    ]

    for copy in away + z_copies + y_copies + m_away:
        copy.wait_send()
    for copy in beside + onward:
        copy.wait_send()
    for copy in m_beside + m_onward + spread:
        copy.wait()


def adjoint_kernel(owner_ref, kern_ref, col_ref, mis_ref, out_ref, acc):
    blocks = col_ref.shape[0]
    levels = kern_ref.shape[1]
    count = acc.shape[0]
    tiles = acc.shape[2] // levels
    acc[...] = jnp.zeros_like(acc)
    lane_row = lax.broadcasted_iota(jnp.int32, (LANES, LANES), 0).astype(F32).astype(BF)
    one, zero = jnp.ones((), BF), jnp.zeros((), BF)

    def step(group, carry):
        base = pl.multiple_of(group * GROUP, GROUP)
        cols = col_ref[pl.ds(base, GROUP), :]
        low = jnp.bitwise_and(cols, LANES - 1).astype(F32)
        high = jnp.right_shift(cols, 7)
        misfit = mis_ref[pl.ds(base, GROUP), :].astype(F32)
        parts = [jnp.where(high == tile, misfit, 0.0) for tile in range(tiles)]
        for i in range(GROUP):
            owner = owner_ref[base + i]
            kern = kern_ref[base + i].astype(F32)
            rows = jnp.concatenate(
                [(kern * part[i : i + 1, :]).astype(BF) for part in parts], axis=0
            )
            row = jnp.broadcast_to(low[i : i + 1, :], (LANES, LANES)).astype(BF)
            hot = jnp.where(lane_row == row, one, zero)
            acc[owner] += lax.dot_general(
                hot, rows, (((1,), (1,)), ((), ())), preferred_element_type=F32
            )
        return carry

    lax.fori_loop(0, blocks // GROUP, step, 0)

    lane = lax.broadcasted_iota(jnp.int32, (levels, LANES), 1)
    sums = [jnp.transpose(acc[h]) for h in range(count)]
    for h in range(count):
        out_ref[h, pl.ds(0, tiles * levels)] = sums[h].astype(BF)
        edge = jnp.zeros((levels, LANES), F32)
        if h < count - 1:
            edge = jnp.where(lane < HALF, sums[h + 1][:levels], edge)
        if h > 0:
            edge = jnp.where(lane >= LANES - HALF, sums[h - 1][(tiles - 1) * levels :], edge)
        out_ref[h, pl.ds(tiles * levels, levels)] = edge.astype(BF)


def return_kernel(count, levs, x_ref, out_ref, slots, send_a, recv_a, send_b, recv_b):
    me, lev = lax.axis_index("horiz"), lax.axis_index("lev")
    peers = others("horiz", count)
    sides = others("lev", levs)
    greet([{"horiz": peer} for peer in peers] + [{"lev": side} for side in sides])
    copies = [
        send(x_ref.at[peer], slots.at[k], send_a.at[k], recv_a.at[k], {"horiz": peer})
        for k, peer in enumerate(peers)
    ]
    total = x_ref[me].astype(F32)
    for k, copy in enumerate(copies):
        copy.wait()
        total = total + slots[k].astype(F32)
    out_ref[lev] = total
    block = out_ref.at[lev]
    copies = [
        send(block, block, send_b.at[k], recv_b.at[k], {"lev": side})
        for k, side in enumerate(sides)
    ]
    for copy in copies:
        copy.wait()


def final_kernel(
    mixed_ref, fg_ref, kron_hbm, hi_ref, lo_ref, control_ref, out_ref, grad_v, kron_ref, sem
):
    levels, members, width = control_ref.shape
    size = levels * PAIR
    at = pl.multiple_of(lax.axis_index("lev") * size, size)
    kron_copy = fetch(kron_hbm.at[pl.ds(at, size)], kron_ref, sem)
    slabs = fg_ref.shape[0]
    tiles = width // LANES + 1
    for half in range(members // PAIR):
        for slab in range(slabs):
            for t in range(tiles):
                fg = fg_ref[slab, pl.ds(t * levels, levels), :]
                m = mixed_ref[half, pl.ds(slab * levels, levels), :, pl.ds(t * LANES, LANES)]
                grad = m.astype(F32) * fg[:, None, :]
                grad_v[pl.ds(slab * levels * PAIR, levels * PAIR), pl.ds(t * LANES, LANES)] = (
                    grad.astype(BF).reshape(levels * PAIR, LANES)
                )
        if half == 0:
            kron_copy.wait()
        mixed_levels = dot(kron_ref[...], grad_v[...])
        high = mixed_levels.astype(BF)
        low = (mixed_levels - high.astype(F32)).astype(BF)
        total = dot(high, hi_ref[...]) + dot(high, lo_ref[...]) + dot(low, hi_ref[...])
        part = pl.ds(half * PAIR, PAIR)
        out_ref[:, part, :] = control_ref[:, part, :] + total.reshape(levels, PAIR, width)


def vmem(count):
    return [pl.BlockSpec(memory_space=pltpu.VMEM)] * count


def smem(count):
    return [pl.BlockSpec(memory_space=pltpu.SMEM)] * count


def hbm(count):
    return [pl.BlockSpec(memory_space=pltpu.HBM)] * count


def pairs(*size):
    return pltpu.SemaphoreType.DMA((2,) + size)


def body(
    control,
    members,
    extinction,
    kernels,
    innovation,
    obs_weight,
    owners,
    pixel_columns,
    pixel_counts,
):
    levels, mem_count, width = control.shape
    blocks, _, pixels = kernels.shape
    count, levs = lax.axis_size("horiz"), lax.axis_size("lev")
    tiles = width // LANES
    halves = mem_count // PAIR
    rows = blocks // levs
    full = width + LANES
    kron_all = spread_levels(level_matrix())
    high, low = tap_matrix(width)
    hi, lo = jnp.asarray(high), jnp.asarray(low)
    hi_t, lo_t = jnp.asarray(high.T), jnp.asarray(low.T)
    scale = 1.0 / math.sqrt(mem_count)
    owner_ids = owners[:, 0]

    misfit, mixed_all = pl.pallas_call(
        functools.partial(front_kernel, levs, count, scale),
        out_shape=[
            jax.ShapeDtypeStruct((blocks, pixels), BF),
            jax.ShapeDtypeStruct((halves, levs * levels, PAIR, full), BF),
        ],
        in_specs=hbm(12),
        out_specs=vmem(2),
        scratch_shapes=[
            pltpu.SMEM(extinction.shape, F32),
            pltpu.SMEM(owner_ids.shape, jnp.int32),
            pltpu.VMEM(control.shape, F32),
            pltpu.VMEM(members.shape, BF),
            pltpu.VMEM(kernels.shape, BF),
            pltpu.VMEM(pixel_columns.shape, jnp.int32),
            pltpu.VMEM((rows, pixels), BF),
            pltpu.VMEM((rows, pixels), BF),
            pltpu.VMEM((levs, rows), jnp.int32),
            pltpu.VMEM((levels * PAIR, LEV * PAIR), BF),
            pltpu.VMEM((width, full), BF),
            pltpu.VMEM((width, full), BF),
            pltpu.VMEM((halves, levs * levels, PAIR, width), BF),
            pltpu.VMEM((levels, mem_count, full), F32),
            pltpu.VMEM((2, halves, levels, PAIR, LANES), BF),
            pltpu.VMEM((halves, levels * PAIR, width), BF),
            pltpu.VMEM((count, tiles + 1, levels, LANES), BF),
            pltpu.VMEM((count, tiles, levels, LANES), F32),
            pltpu.VMEM((blocks, pixels), F32),
            pltpu.VMEM((levs - 1, rows, pixels), F32),
            pltpu.SemaphoreType.DMA((11,)),
            pltpu.SemaphoreType.DMA((tiles,)),
            pairs(tiles),
            pairs(tiles),
            pairs(tiles),
            pairs(2),
            pairs(count // 2 - 1),
            pairs(count // 2),
            pairs(levs - 1),
            pairs(levs - 1),
            pairs(halves),
            pairs(halves),
            pairs(halves),
        ],
        compiler_params=pltpu.CompilerParams(
            vmem_limit_bytes=58 * MIB, collective_id=0, has_side_effects=True
        ),
    )(
        extinction,
        owner_ids,
        control,
        members,
        kernels,
        pixel_columns,
        innovation,
        obs_weight,
        pixel_counts.reshape(levs, rows),
        kron_all,
        hi_t,
        lo_t,
    )

    partial = pl.pallas_call(
        adjoint_kernel,
        out_shape=jax.ShapeDtypeStruct((count, (tiles + 1) * levels, LANES), BF),
        in_specs=smem(1) + vmem(3),
        out_specs=pl.BlockSpec(memory_space=pltpu.VMEM),
        scratch_shapes=[pltpu.VMEM((count, LANES, tiles * levels), F32)],
        compiler_params=pltpu.CompilerParams(vmem_limit_bytes=32 * MIB),
    )(owner_ids, kernels, pixel_columns, misfit)

    fg_all = pl.pallas_call(
        functools.partial(return_kernel, count, levs),
        out_shape=jax.ShapeDtypeStruct((levs, (tiles + 1) * levels, LANES), F32),
        in_specs=vmem(1),
        out_specs=pl.BlockSpec(memory_space=pltpu.VMEM),
        scratch_shapes=[pltpu.VMEM((count - 1, (tiles + 1) * levels, LANES), BF)]
        + [pltpu.SemaphoreType.DMA((count - 1,))] * 2
        + [pltpu.SemaphoreType.DMA((levs - 1,))] * 2,
        compiler_params=pltpu.CompilerParams(
            vmem_limit_bytes=32 * MIB, collective_id=1, has_side_effects=True
        ),
    )(partial)

    return pl.pallas_call(
        final_kernel,
        out_shape=jax.ShapeDtypeStruct(control.shape, F32),
        in_specs=vmem(2) + hbm(1) + vmem(3),
        out_specs=pl.BlockSpec(memory_space=pltpu.VMEM),
        scratch_shapes=[
            pltpu.VMEM((LEV * PAIR, full), BF),
            pltpu.VMEM((levels * PAIR, LEV * PAIR), BF),
            pltpu.SemaphoreType.DMA,
        ],
        compiler_params=pltpu.CompilerParams(vmem_limit_bytes=32 * MIB),
    )(mixed_all, fg_all, kron_all, hi, lo, control)


def solution(mesh):
    placed = (
        P("lev", None, "horiz"),
        P("lev", None, None, "horiz"),
        P(),
        P("horiz", "lev", None),
        P("horiz", None),
        P("horiz", None),
        P("horiz", None),
        P("horiz", None),
        P("horiz"),
    )
    return jax.shard_map(
        body, mesh=mesh, in_specs=placed, out_specs=P("lev", None, "horiz"), check_vma=False
    )
```

time: 108 us -> 72.6 us (0.67)
  between operations: 13.7 us -> 0.12 us
  Pallas kernels: 80 us -> 69.5 us
  local copies, waits for them, and re-layouts: 12.9 us -> 2.81 us
    pallas_call x9 -> x4, Pallas kernels: 80 us -> 69.5 us  [the longest x1 49.4 us: body(): pl.pallas_call(functools.partial(front_kernel, levs, count, scale), out_s...]
    unnamed x34 -> x18, local copies, waits for them, and re-layouts: 9.76 us -> 2.81 us
    dynamic_slice x1 -> x0, local copies, waits for them, and re-layouts: 1.08 us -> none  [body(): lax.dynamic_slice_in_dim(spread_levels(level_loc), first * PAIR, levels *...]
  transfers between devices with their start and end apart: 1 -> 0, of which waited for: 0 -> 0; matrix products, arithmetic and copies ran while one was open for 3% -> 0% of each run, Pallas kernels for 45% -> 0%
where the time goes in v1:
time: 72.6 us; the launch traced here: 72.4 us
  Pallas kernels  69.5 us (96%)
  local copies, waits for them, and re-layouts  2.81 us (4%)
    pallas_call x1, Pallas kernels, body(): pl.pallas_call(functools.partial(front_kernel, levs, count, scale), out_s...  49.4 us
    pallas_call x1, Pallas kernels, body(): pl.pallas_call(functools.partial(return_kernel, count, levs), out_shape=j...  9.81 us
    pallas_call x1, Pallas kernels, body(): pl.pallas_call(adjoint_kernel, out_shape=jax.ShapeDtypeStruct((count, (ti...  6.58 us
    pallas_call x1, Pallas kernels, body(): pl.pallas_call(final_kernel, out_shape=jax.ShapeDtypeStruct(control.shape...  3.68 us
    unnamed x18, local copies, waits for them, and re-layouts  2.81 us

profile of v1, /device:TPU:0, one launch (start us, length us, event | category | flops | bytes accessed | tf_op | source)
XLA Modules:
  0.0 72.4 jit_solution(10548935592424549173)
XLA Ops:
  0.0 0.0 copy-start
  0.0 0.0 copy-start.4
  0.0 0.0 copy-start.8
  0.0 0.0 copy-start.2
  0.0 0.0 copy-start.6
  0.0 49.4 %shard_map.136 = (bf16[512,128]{1,0:T(8,128)(2,1)}, bf16[2,64,16,640]{3,2,1,0:T(8,128)(2,1)}) custom-call(f32[4]{0:T(128)} %ext_hbm.1, s32[512]{0:T(512)} %bitcast.2, f32[16,32,512]{2,1,0:T(8,128)} %control_ref.1, bf16[16,4,32,512]{3,2,1,0:T(8,128)(2,1)} %members_hbm.1, bf16[512,16,128]{2,1,0:T(8,128)(2,1)} %kern_ref.1, s32[512,128]{1,0:T(8,128)} %col_ref.1, ...), custom_call_target="tpu_custom_call" | custom-call | tf_op jit(solution)/shard_map/pallas_call | solution.py:511
  49.4 0.0 copy-start.1
  49.4 0.0 copy-start.5
  49.4 0.0 copy-done
  49.5 0.0 copy-done.4
  49.5 0.0 copy-done.8
  49.5 0.0 copy-start.7
  49.5 1.0 %copy-done.7 = bf16[512,128]{1,0:T(8,128)(2,1)S(1)} copy-done((bf16[512,128]{1,0:T(8,128)(2,1)S(1)}, bf16[512,128]{1,0:T(8,128)(2,1)}, u32[]{:S(2)}) %copy-start.7) | copy-done | bytes 131096
  50.5 6.6 %shard_map.137.x_ref = bf16[8,80,128]{2,1,0:T(8,128)(2,1)S(1)} custom-call(s32[512]{0:T(512)S(1)} %bitcast.3, bf16[512,16,128]{2,1,0:T(8,128)(2,1)S(1)} %copy-done, s32[512,128]{1,0:T(8,128)S(1)} %copy-done.4, bf16[512,128]{1,0:T(8,128)(2,1)S(1)} %copy-done.7), custom_call_target="tpu_custom_call" | custom-call | tf_op jit(solution)/shard_map/pallas_call | solution.py:572
  57.1 9.8 %shard_map.138.fg_ref = f32[4,80,128]{2,1,0:T(8,128)S(1)} custom-call(bf16[8,80,128]{2,1,0:T(8,128)(2,1)S(1)} %shard_map.137.x_ref), custom_call_target="tpu_custom_call" | custom-call | tf_op jit(solution)/shard_map/pallas_call | solution.py:581
  66.9 0.0 copy-done.2
  67.0 0.0 copy-done.6
  67.0 0.0 copy-done.1
  67.0 0.0 copy-done.5
  67.0 0.0 copy-start.3
  67.0 1.7 %copy-done.3 = bf16[2,64,16,640]{3,2,1,0:T(8,128)(2,1)S(1)} copy-done((bf16[2,64,16,640]{3,2,1,0:T(8,128)(2,1)S(1)}, bf16[2,64,16,640]{3,2,1,0:T(8,128)(2,1)}, u32[]{:S(2)}) %copy-start.3) | copy-done | bytes 2621464
  68.7 3.7 %shard_map.139 = f32[16,32,512]{2,1,0:T(8,128)} custom-call(bf16[2,64,16,640]{3,2,1,0:T(8,128)(2,1)S(1)} %copy-done.3, f32[4,80,128]{2,1,0:T(8,128)S(1)} %shard_map.138.fg_ref, bf16[1024,1024]{1,0:T(8,128)(2,1)S(1)} %copy-done.1, bf16[640,512]{1,0:T(8,128)(2,1)S(1)} %copy-done.6, bf16[640,512]{1,0:T(8,128)(2,1)S(1)} %copy-done.5, f32[16,32,512]{2,1,0:T(8,128)S(1)} %copy-done.2), custom_call_target="tpu_custom_call" | custom-call | tf_op jit(solution)/shard_map/pallas_call | solution.py:594
Async XLA Ops:
  0.0 49.5 %copy-start = (bf16[512,16,128]{2,1,0:T(8,128)(2,1)S(1)}, bf16[512,16,128]{2,1,0:T(8,128)(2,1)}, u32[]{:S(2)}) copy-start(bf16[512,16,128]{2,1,0:T(8,128)(2,1)} %kern_ref.1) | copy-start | bytes 6291460
  0.0 49.5 %copy-start.4 = (s32[512,128]{1,0:T(8,128)S(1)}, s32[512,128]{1,0:T(8,128)}, u32[]{:S(2)}) copy-start(s32[512,128]{1,0:T(8,128)} %col_ref.1) | copy-start | bytes 786436
  0.0 49.5 %copy-start.8 = (s32[512,1]{0,1:T(1,128)S(1)}, s32[512,1]{0,1:T(1,128)}, u32[]{:S(2)}) copy-start(s32[512,1]{0,1:T(1,128)} %param.20) | copy-start | bytes 6148
  0.0 66.9 %copy-start.2 = (f32[16,32,512]{2,1,0:T(8,128)S(1)}, f32[16,32,512]{2,1,0:T(8,128)}, u32[]{:S(2)}) copy-start(f32[16,32,512]{2,1,0:T(8,128)} %control_ref.1) | copy-start | bytes 3145732
  0.0 66.9 %copy-start.6 = (bf16[640,512]{1,0:T(8,128)(2,1)S(1)}, bf16[640,512]{1,0:T(8,128)(2,1)}, u32[]{:S(2)}) copy-start(bf16[640,512]{1,0:T(8,128)(2,1)} %constant.11.clone.hi_ref) | copy-start | bytes 1966084
  49.4 17.5 %copy-start.1 = (bf16[1024,1024]{1,0:T(8,128)(2,1)S(1)}, bf16[1024,1024]{1,0:T(8,128)(2,1)}, u32[]{:S(2)}) copy-start(bf16[1024,1024]{1,0:T(8,128)(2,1)} %constant.10.clone.kron_hbm) | copy-start | bytes 6291460
  49.4 17.5 %copy-start.5 = (bf16[640,512]{1,0:T(8,128)(2,1)S(1)}, bf16[640,512]{1,0:T(8,128)(2,1)}, u32[]{:S(2)}) copy-start(bf16[640,512]{1,0:T(8,128)(2,1)} %constant.12.clone.lo_ref) | copy-start | bytes 1966084
  49.5 1.1 %copy-start.7 = (bf16[512,128]{1,0:T(8,128)(2,1)S(1)}, bf16[512,128]{1,0:T(8,128)(2,1)}, u32[]{:S(2)}) copy-start(bf16[512,128]{1,0:T(8,128)(2,1)} %get-tuple-element.8.mis_ref) | copy-start | bytes 393220
  67.0 1.7 %copy-start.3 = (bf16[2,64,16,640]{3,2,1,0:T(8,128)(2,1)S(1)}, bf16[2,64,16,640]{3,2,1,0:T(8,128)(2,1)}, u32[]{:S(2)}) copy-start(bf16[2,64,16,640]{3,2,1,0:T(8,128)(2,1)} %get-tuple-element.7.mixed_ref) | copy-start | bytes 7864324

commit v2 on v1

--- a/solution.py
+++ b/solution.py
@@ -127,11 +127,13 @@
     lo_v,
     ctrl_all,
     mixed_v,
+    mixed_own,
     halo_v,
     vert_v,
     field_all,
     field_v,
     part_v,
+    part_b,
     slots,
     local_sem,
     ctl_sem,
@@ -139,13 +141,13 @@
     c_near,
     c_on,
     h_sem,
-    z_sem,
-    y_sem,
+    f_sem,
     t_sem,
     g_sem,
     m_far,
     m_near,
     m_on,
+    m_loc,
 ):
     levels, members, width = control_v.shape
     tiles = width // LANES
@@ -209,13 +211,13 @@
             total = total + ext_s[species] * members_v[:, species, :, tile_cols[t]].astype(F32)
         mixed_v[:, :, tile_cols[t]] = total
         for half in range(halves):
-            mixed_all[half, own, :, tile_cols[t]] = total[:, half * PAIR : (half + 1) * PAIR].astype(BF)
+            mixed_own[half, :, :, tile_cols[t]] = total[:, half * PAIR : (half + 1) * PAIR].astype(BF)
 
     mix(0)
     mix(tiles - 1)
     edges = [
         send(
-            mixed_all.at[:, own, :, tile_cols[t]],
+            mixed_own.at[:, :, :, tile_cols[t]],
             halo_v.at[k],
             h_sem.at[0, k],
             h_sem.at[1, k],
@@ -243,12 +245,21 @@
         halo = jnp.where(lane < after, halo_v[0, half].astype(F32), 0.0)
         halo = jnp.where(lane >= before, halo_v[1, half].astype(F32), halo)
         mixed_v[:, pl.ds(half * PAIR, PAIR), pl.ds(width, LANES)] = halo
-        mixed_all[half, own, :, pl.ds(width, LANES)] = halo.astype(BF)
-
+        mixed_own[half, :, :, pl.ds(width, LANES)] = halo.astype(BF)
+
+    m_away, m_beside, m_onward, m_kept = [], [], [], []
     local[2].wait()
     for t, c in enumerate(tile_cols):
         if t:
             pass_on(t)
+        if t == tiles - 1:
+            for half in range(halves):
+                block, place = mixed_own.at[half], mixed_all.at[half, own]
+                m_away.append(send(block, place, m_far.at[0, half], m_far.at[1, half], {"lev": far}))
+                m_beside.append(
+                    send(block, place, m_near.at[0, half], m_near.at[1, half], {"lev": near})
+                )
+                m_kept.append(fetch(block, place, m_loc.at[half]))
         beside[t].wait_recv()
         onward[t].wait_recv()
         for half in range(halves):
@@ -268,27 +279,12 @@
     for t in range(tiles + 1):
         field_all[me, t] = total[:, t * LANES : (t + 1) * LANES].astype(BF)
 
-    beyond = [lax.rem(me + 2 * k, count) for k in range(1, count // 2)]
-    beyond_from = [lax.rem(me + count - 2 * k, count) for k in range(1, count // 2)]
-    pair = flip(me)
     block = field_all.at[me]
-    z_copies = [
-        send(block, block, z_sem.at[0, k], z_sem.at[1, k], {"horiz": peer})
-        for k, peer in enumerate(beyond)
-    ]
-    y_copies = [send(block, block, y_sem.at[0, 0], y_sem.at[1, 0], {"horiz": pair})]
-    for k, peer in enumerate(beyond_from):
-        z_copies[k].wait_recv()
-        block = field_all.at[peer]
-        y_copies.append(send(block, block, y_sem.at[0, k + 1], y_sem.at[1, k + 1], {"horiz": pair}))
-
-    m_away, m_beside, m_onward = [], [], []
-    for half in range(halves):
-        block = mixed_all.at[half, own]
-        m_away.append(send(block, block, m_far.at[0, half], m_far.at[1, half], {"lev": far}))
-        m_beside.append(send(block, block, m_near.at[0, half], m_near.at[1, half], {"lev": near}))
-
-    for copy in y_copies:
+    f_copies = [
+        send(block, block, f_sem.at[0, k], f_sem.at[1, k], {"horiz": peer})
+        for k, peer in enumerate(others("horiz", count))
+    ]
+    for copy in f_copies:
         copy.wait_recv()
     lane2 = lax.broadcasted_iota(jnp.int32, (levels, LANES), 1)
     for h in range(count):
@@ -324,7 +320,9 @@
                     picked = jnp.where(high == tile, other, picked)
                 prod = picked * kern_v[base + i].astype(F32)
                 out.append(jnp.sum(prod, axis=0, keepdims=True))
-            part_v[pl.ds(base, GROUP), :] = jnp.concatenate(out, axis=0)
+            rows_sum = jnp.concatenate(out, axis=0)
+            part_v[pl.ds(base, GROUP), :] = rows_sum
+            part_b[pl.ds(base, GROUP), :] = rows_sum.astype(BF)
             return carry
 
         lax.fori_loop(0, rows // GROUP, step, 0)
@@ -332,7 +330,7 @@
         @pl.when(k < levs - 1)
         def _():
             remote(
-                part_v.at[pl.ds(start, rows)], slots.at[k], t_sem.at[0, k], t_sem.at[1, k], {"lev": peer}
+                part_b.at[pl.ds(start, rows)], slots.at[k], t_sem.at[0, k], t_sem.at[1, k], {"lev": peer}
             ).start()
 
         return carry
@@ -353,10 +351,10 @@
     for k, side in enumerate(sides):
         start = pl.multiple_of(side * rows, rows)
         copy = remote(
-            part_v.at[pl.ds(start, rows)], slots.at[k], t_sem.at[0, k], t_sem.at[1, k], {"lev": side}
+            part_b.at[pl.ds(start, rows)], slots.at[k], t_sem.at[0, k], t_sem.at[1, k], {"lev": side}
         )
         copy.wait()
-        total = total + slots[k]
+        total = total + slots[k].astype(F32)
     misfit = w_v[...].astype(F32) * (total - inn_v[...].astype(F32)) * scale
     misfit_ref[mine, :] = jnp.where(live, misfit, 0.0).astype(BF)
     block = misfit_ref.at[mine]
@@ -365,11 +363,11 @@
         for k, side in enumerate(sides)
     ]
 
-    for copy in away + z_copies + y_copies + m_away:
+    for copy in away + f_copies + m_away:
         copy.wait_send()
     for copy in beside + onward:
         copy.wait_send()
-    for copy in m_beside + m_onward + spread:
+    for copy in m_beside + m_onward + m_kept + spread:
         copy.wait()
 
 
@@ -416,55 +414,90 @@
         out_ref[h, pl.ds(tiles * levels, levels)] = edge.astype(BF)
 
 
-def return_kernel(count, levs, x_ref, out_ref, slots, send_a, recv_a, send_b, recv_b):
+def back_kernel(
+    count,
+    levs,
+    x_ref,
+    mixed_hbm,
+    kron_hbm,
+    hi_hbm,
+    lo_hbm,
+    out_ref,
+    mixed_v,
+    kron_v,
+    hi_v,
+    lo_v,
+    fg_v,
+    levels_v,
+    slots,
+    r_sem,
+    a_sem,
+    local_sem,
+):
+    levels, members, width = out_ref.shape
+    halves = members // PAIR
+    size = levels * PAIR
+    tiles = width // LANES + 1
     me, lev = lax.axis_index("horiz"), lax.axis_index("lev")
+    near, far = flip(lev), lax.rem(lev + 2, levs)
+    across = flip(far)
+    at = pl.multiple_of(lev * size, size)
+    local = [
+        fetch(src, dst, local_sem.at[k])
+        for k, (src, dst) in enumerate(
+            [
+                (mixed_hbm, mixed_v),
+                (kron_hbm.at[pl.ds(at, size)], kron_v),
+                (hi_hbm, hi_v),
+                (lo_hbm, lo_v),
+            ]
+        )
+    ]
     peers = others("horiz", count)
-    sides = others("lev", levs)
+    sides = [near, far, across]
     greet([{"horiz": peer} for peer in peers] + [{"lev": side} for side in sides])
-    copies = [
-        send(x_ref.at[peer], slots.at[k], send_a.at[k], recv_a.at[k], {"horiz": peer})
+    reduce = [
+        send(x_ref.at[peer], slots.at[k], r_sem.at[0, k], r_sem.at[1, k], {"horiz": peer})
         for k, peer in enumerate(peers)
     ]
     total = x_ref[me].astype(F32)
-    for k, copy in enumerate(copies):
+    for k, copy in enumerate(reduce):
+        copy.wait_recv()
+        total = total + slots[k].astype(F32)
+    fg_v[lev] = total
+    block = fg_v.at[lev]
+    spread = [
+        send(block, block, a_sem.at[0, k], a_sem.at[1, k], {"lev": side})
+        for k, side in enumerate(sides)
+    ]
+    for copy in local:
         copy.wait()
-        total = total + slots[k].astype(F32)
-    out_ref[lev] = total
-    block = out_ref.at[lev]
-    copies = [
-        send(block, block, send_b.at[k], recv_b.at[k], {"lev": side})
-        for k, side in enumerate(sides)
-    ]
-    for copy in copies:
-        copy.wait()
-
-
-def final_kernel(
-    mixed_ref, fg_ref, kron_hbm, hi_ref, lo_ref, control_ref, out_ref, grad_v, kron_ref, sem
-):
-    levels, members, width = control_ref.shape
-    size = levels * PAIR
-    at = pl.multiple_of(lax.axis_index("lev") * size, size)
-    kron_copy = fetch(kron_hbm.at[pl.ds(at, size)], kron_ref, sem)
-    slabs = fg_ref.shape[0]
-    tiles = width // LANES + 1
-    for half in range(members // PAIR):
-        for slab in range(slabs):
+
+    def slab(index, first):
+        start = pl.multiple_of(index * levels, levels)
+        begin = pl.multiple_of(index * size, size)
+        for half in range(halves):
+            columns = []
             for t in range(tiles):
-                fg = fg_ref[slab, pl.ds(t * levels, levels), :]
-                m = mixed_ref[half, pl.ds(slab * levels, levels), :, pl.ds(t * LANES, LANES)]
+                fg = fg_v[index, pl.ds(t * levels, levels), :]
+                m = mixed_v[half, pl.ds(start, levels), :, pl.ds(t * LANES, LANES)]
                 grad = m.astype(F32) * fg[:, None, :]
-                grad_v[pl.ds(slab * levels * PAIR, levels * PAIR), pl.ds(t * LANES, LANES)] = (
-                    grad.astype(BF).reshape(levels * PAIR, LANES)
-                )
-        if half == 0:
-            kron_copy.wait()
-        mixed_levels = dot(kron_ref[...], grad_v[...])
+                columns.append(grad.astype(BF).reshape(size, LANES))
+            term = dot(kron_v[:, pl.ds(begin, size)], jnp.concatenate(columns, axis=1))
+            levels_v[half] = term if first else levels_v[half] + term
+
+    slab(lev, True)
+    for k, side in enumerate(sides):
+        spread[k].wait_recv()
+        slab(side, False)
+    for half in range(halves):
+        mixed_levels = levels_v[half]
         high = mixed_levels.astype(BF)
         low = (mixed_levels - high.astype(F32)).astype(BF)
-        total = dot(high, hi_ref[...]) + dot(high, lo_ref[...]) + dot(low, hi_ref[...])
-        part = pl.ds(half * PAIR, PAIR)
-        out_ref[:, part, :] = control_ref[:, part, :] + total.reshape(levels, PAIR, width)
+        total = dot(high, hi_v[...]) + dot(high, lo_v[...]) + dot(low, hi_v[...])
+        out_ref[:, pl.ds(half * PAIR, PAIR), :] = total.reshape(levels, PAIR, width)
+    for copy in reduce + spread:
+        copy.wait_send()
 
 
 def vmem(count):
@@ -515,7 +548,7 @@
             jax.ShapeDtypeStruct((halves, levs * levels, PAIR, full), BF),
         ],
         in_specs=hbm(12),
-        out_specs=vmem(2),
+        out_specs=vmem(1) + hbm(1),
         scratch_shapes=[
             pltpu.SMEM(extinction.shape, F32),
             pltpu.SMEM(owner_ids.shape, jnp.int32),
@@ -531,25 +564,27 @@
             pltpu.VMEM((width, full), BF),
             pltpu.VMEM((halves, levs * levels, PAIR, width), BF),
             pltpu.VMEM((levels, mem_count, full), F32),
+            pltpu.VMEM((halves, levels, PAIR, full), BF),
             pltpu.VMEM((2, halves, levels, PAIR, LANES), BF),
             pltpu.VMEM((halves, levels * PAIR, width), BF),
             pltpu.VMEM((count, tiles + 1, levels, LANES), BF),
             pltpu.VMEM((count, tiles, levels, LANES), F32),
             pltpu.VMEM((blocks, pixels), F32),
-            pltpu.VMEM((levs - 1, rows, pixels), F32),
+            pltpu.VMEM((blocks, pixels), BF),
+            pltpu.VMEM((levs - 1, rows, pixels), BF),
             pltpu.SemaphoreType.DMA((11,)),
             pltpu.SemaphoreType.DMA((tiles,)),
             pairs(tiles),
             pairs(tiles),
             pairs(tiles),
             pairs(2),
-            pairs(count // 2 - 1),
-            pairs(count // 2),
+            pairs(count - 1),
             pairs(levs - 1),
             pairs(levs - 1),
             pairs(halves),
             pairs(halves),
             pairs(halves),
+            pltpu.SemaphoreType.DMA((halves,)),
         ],
         compiler_params=pltpu.CompilerParams(
             vmem_limit_bytes=58 * MIB, collective_id=0, has_side_effects=True
@@ -578,31 +613,28 @@
         compiler_params=pltpu.CompilerParams(vmem_limit_bytes=32 * MIB),
     )(owner_ids, kernels, pixel_columns, misfit)
 
-    fg_all = pl.pallas_call(
-        functools.partial(return_kernel, count, levs),
-        out_shape=jax.ShapeDtypeStruct((levs, (tiles + 1) * levels, LANES), F32),
-        in_specs=vmem(1),
-        out_specs=pl.BlockSpec(memory_space=pltpu.VMEM),
-        scratch_shapes=[pltpu.VMEM((count - 1, (tiles + 1) * levels, LANES), BF)]
-        + [pltpu.SemaphoreType.DMA((count - 1,))] * 2
-        + [pltpu.SemaphoreType.DMA((levs - 1,))] * 2,
-        compiler_params=pltpu.CompilerParams(
-            vmem_limit_bytes=32 * MIB, collective_id=1, has_side_effects=True
-        ),
-    )(partial)
-
-    return pl.pallas_call(
-        final_kernel,
+    delta = pl.pallas_call(
+        functools.partial(back_kernel, count, levs),
         out_shape=jax.ShapeDtypeStruct(control.shape, F32),
-        in_specs=vmem(2) + hbm(1) + vmem(3),
+        in_specs=vmem(1) + hbm(4),
         out_specs=pl.BlockSpec(memory_space=pltpu.VMEM),
         scratch_shapes=[
-            pltpu.VMEM((LEV * PAIR, full), BF),
+            pltpu.VMEM(mixed_all.shape, BF),
             pltpu.VMEM((levels * PAIR, LEV * PAIR), BF),
-            pltpu.SemaphoreType.DMA,
+            pltpu.VMEM((full, width), BF),
+            pltpu.VMEM((full, width), BF),
+            pltpu.VMEM((levs, (tiles + 1) * levels, LANES), F32),
+            pltpu.VMEM((halves, levels * PAIR, full), F32),
+            pltpu.VMEM((count - 1, (tiles + 1) * levels, LANES), BF),
+            pairs(count - 1),
+            pairs(levs - 1),
+            pltpu.SemaphoreType.DMA((4,)),
         ],
-        compiler_params=pltpu.CompilerParams(vmem_limit_bytes=32 * MIB),
-    )(mixed_all, fg_all, kron_all, hi, lo, control)
+        compiler_params=pltpu.CompilerParams(
+            vmem_limit_bytes=48 * MIB, collective_id=1, has_side_effects=True
+        ),
+    )(partial, mixed_all, kron_all, hi, lo)
+    return control + delta
 
 
 def solution(mesh):

time: 72.6 us -> 62.1 us (0.86)
  Pallas kernels: 69.5 us -> 59.5 us
  local copies, waits for them, and re-layouts: 2.81 us -> 1.07 us
  other arithmetic: 0 us -> 1.21 us
    pallas_call x1, Pallas kernels: 49.4 us -> 40.9 us  [body(): pl.pallas_call(functools.partial(front_kernel, levs, count, scale), out_s...]
    unnamed x18 -> x16, local copies, waits for them, and re-layouts: 2.81 us -> 1.07 us
    pallas_call x2 -> x1, Pallas kernels: 13.5 us -> 12.1 us  [body(): pl.pallas_call(functools.partial(back_kernel, count, levs), out_shape=jax...]
    add x0 -> x1, other arithmetic: none -> 1.21 us  [body(): return control + delta]
where the time goes in v2:
time: 62.1 us; the launch traced here: 61.9 us
  Pallas kernels  59.5 us (96%)
  other arithmetic  1.21 us (2%)
  local copies, waits for them, and re-layouts  1.07 us (2%)
    pallas_call x1, Pallas kernels, body(): pl.pallas_call(functools.partial(front_kernel, levs, count, scale), out_s...  40.9 us
    pallas_call x1, Pallas kernels, body(): pl.pallas_call(functools.partial(back_kernel, count, levs), out_shape=jax...  12.1 us
    pallas_call x1, Pallas kernels, body(): pl.pallas_call(adjoint_kernel, out_shape=jax.ShapeDtypeStruct((count, (ti...  6.58 us

profile of v2, /device:TPU:0, one launch (start us, length us, event | category | flops | bytes accessed | tf_op | source)
XLA Modules:
  0.0 61.9 jit_solution(15584655637510124984)
XLA Ops:
  0.0 0.0 copy-start.1
  0.0 0.0 copy-start.2
  0.0 0.0 copy-start.6
  0.0 0.0 copy-start.3
  0.0 0.0 copy-start.4
  0.0 40.9 %shard_map.136 = (bf16[512,128]{1,0:T(8,128)(2,1)}, bf16[2,64,16,640]{3,2,1,0:T(8,128)(2,1)}) custom-call(f32[4]{0:T(128)} %ext_hbm.1, s32[512]{0:T(512)} %bitcast.2, f32[16,32,512]{2,1,0:T(8,128)} %control_hbm.1, bf16[16,4,32,512]{3,2,1,0:T(8,128)(2,1)} %members_hbm.1, bf16[512,16,128]{2,1,0:T(8,128)(2,1)} %kern_ref.1, s32[512,128]{1,0:T(8,128)} %col_ref.1, ...), custom_call_target="tpu_custom_call" | custom-call | tf_op jit(solution)/shard_map/pallas_call | solution.py:544
  40.9 0.0 copy-start
  40.9 0.0 copy-done.1
  40.9 0.0 copy-done.2
  40.9 0.0 copy-done.6
  40.9 0.0 copy-start.5
  40.9 1.0 %copy-done.5 = bf16[512,128]{1,0:T(8,128)(2,1)S(1)} copy-done((bf16[512,128]{1,0:T(8,128)(2,1)S(1)}, bf16[512,128]{1,0:T(8,128)(2,1)}, u32[]{:S(2)}) %copy-start.5) | copy-done | bytes 131096
  42.0 6.6 %shard_map.137.x_ref = bf16[8,80,128]{2,1,0:T(8,128)(2,1)S(1)} custom-call(s32[512]{0:T(512)S(1)} %bitcast.3, bf16[512,16,128]{2,1,0:T(8,128)(2,1)S(1)} %copy-done.1, s32[512,128]{1,0:T(8,128)S(1)} %copy-done.2, bf16[512,128]{1,0:T(8,128)(2,1)S(1)} %copy-done.5), custom_call_target="tpu_custom_call" | custom-call | tf_op jit(solution)/shard_map/pallas_call | solution.py:607
  48.6 0.0 copy-done.3
  48.6 0.0 copy-done.4
  48.6 0.0 copy-done
  48.6 0.0 copy-start.7
  48.6 12.1 %shard_map.138 = f32[16,32,512]{2,1,0:T(8,128)S(1)} custom-call(bf16[8,80,128]{2,1,0:T(8,128)(2,1)S(1)} %shard_map.137.x_ref, bf16[2,64,16,640]{3,2,1,0:T(8,128)(2,1)} %get-tuple-element.8.mixed_hbm, bf16[1024,1024]{1,0:T(8,128)(2,1)S(1)} %copy-done, bf16[640,512]{1,0:T(8,128)(2,1)S(1)} %copy-done.4, bf16[640,512]{1,0:T(8,128)(2,1)S(1)} %copy-done.3), custom_call_target="tpu_custom_call" | custom-call | tf_op jit(solution)/shard_map/pallas_call | solution.py:616
  60.7 0.0 copy-done.7
  60.7 1.2 %add.3 = f32[16,32,512]{2,1,0:T(8,128)} add(f32[16,32,512]{2,1,0:T(8,128)S(1)} %copy-done.7, f32[16,32,512]{2,1,0:T(8,128)S(1)} %shard_map.138) | non-fusion elementwise | flops 262144 | bytes 3145728 | tf_op jit(solution)/shard_map/add | solution.py:637
Async XLA Ops:
  0.0 40.9 %copy-start.1 = (bf16[512,16,128]{2,1,0:T(8,128)(2,1)S(1)}, bf16[512,16,128]{2,1,0:T(8,128)(2,1)}, u32[]{:S(2)}) copy-start(bf16[512,16,128]{2,1,0:T(8,128)(2,1)} %kern_ref.1) | copy-start | bytes 6291460
  0.0 40.9 %copy-start.2 = (s32[512,128]{1,0:T(8,128)S(1)}, s32[512,128]{1,0:T(8,128)}, u32[]{:S(2)}) copy-start(s32[512,128]{1,0:T(8,128)} %col_ref.1) | copy-start | bytes 786436
  0.0 40.9 %copy-start.6 = (s32[512,1]{0,1:T(1,128)S(1)}, s32[512,1]{0,1:T(1,128)}, u32[]{:S(2)}) copy-start(s32[512,1]{0,1:T(1,128)} %param.20) | copy-start | bytes 6148
  0.0 48.6 %copy-start.3 = (bf16[640,512]{1,0:T(8,128)(2,1)S(1)}, bf16[640,512]{1,0:T(8,128)(2,1)}, u32[]{:S(2)}) copy-start(bf16[640,512]{1,0:T(8,128)(2,1)} %constant.12.clone.lo_hbm) | copy-start | bytes 1966084
  0.0 48.6 %copy-start.4 = (bf16[640,512]{1,0:T(8,128)(2,1)S(1)}, bf16[640,512]{1,0:T(8,128)(2,1)}, u32[]{:S(2)}) copy-start(bf16[640,512]{1,0:T(8,128)(2,1)} %constant.11.clone.hi_hbm) | copy-start | bytes 1966084
  40.9 7.7 %copy-start = (bf16[1024,1024]{1,0:T(8,128)(2,1)S(1)}, bf16[1024,1024]{1,0:T(8,128)(2,1)}, u32[]{:S(2)}) copy-start(bf16[1024,1024]{1,0:T(8,128)(2,1)} %constant.10.clone.kron_hbm) | copy-start | bytes 6291460
  40.9 1.0 %copy-start.5 = (bf16[512,128]{1,0:T(8,128)(2,1)S(1)}, bf16[512,128]{1,0:T(8,128)(2,1)}, u32[]{:S(2)}) copy-start(bf16[512,128]{1,0:T(8,128)(2,1)} %get-tuple-element.7.mis_ref) | copy-start | bytes 393220
  48.6 12.1 %copy-start.7 = (f32[16,32,512]{2,1,0:T(8,128)S(1)}, f32[16,32,512]{2,1,0:T(8,128)}, u32[]{:S(2)}) copy-start(f32[16,32,512]{2,1,0:T(8,128)} %control_hbm.1) | copy-start | bytes 3145732

commit v3 on v2

v3 whole, which is shorter than its diff:
```python
import functools
import math

import jax
import jax.numpy as jnp
import numpy as np
from jax import lax
from jax.experimental import pallas as pl
from jax.experimental.pallas import tpu as pltpu
from jax.sharding import PartitionSpec as P

LEV = 64
HALF = 4
LANES = 128
PAIR = 16
GROUP = 128
MANY = 128
BF = jnp.bfloat16
F32 = jnp.float32
MESH = pl.DeviceIdType.MESH
MIB = 1024 * 1024


def level_matrix():
    index_levels = np.arange(LEV, dtype=np.float32)
    spread = np.float32(LEV / 8.0)
    distance = index_levels[:, None] - index_levels[None, :]
    matrix = np.exp(-distance * distance / (2 * spread * spread)) / (np.float32(2.5066283) * spread)
    return matrix.astype(BF)


def column_taps():
    offsets = np.arange(2 * HALF + 1, dtype=np.float32) - HALF
    spread = np.float32(HALF / 2.0)
    weights = np.exp(-offsets * offsets / (2 * spread * spread))
    return weights / np.sum(weights)


def tap_matrix(width):
    rows = np.arange(width + LANES)
    place = np.where(rows < width + HALF, rows, rows - width - 2 * HALF)
    used = rows < width + 2 * HALF
    gap = place[:, None] - np.arange(width)[None, :]
    near = (np.abs(gap) <= HALF) & used[:, None]
    dense = np.where(near, column_taps()[np.clip(gap + HALF, 0, 2 * HALF)], 0.0).astype(np.float32)
    high = dense.astype(BF)
    low = (dense - high.astype(np.float32)).astype(BF)
    return high, low


def spread_levels(matrix):
    dense = np.kron(matrix.astype(np.float32), np.eye(PAIR, dtype=np.float32))
    return jnp.asarray(dense.astype(BF))


def dot(a, b):
    return jnp.dot(a, b, preferred_element_type=F32)


def greet(partners):
    barrier = pltpu.get_barrier_semaphore()
    for device in partners:
        pl.semaphore_signal(barrier, inc=1, device_id=device, device_id_type=MESH)
    return lambda: pl.semaphore_wait(barrier, len(partners))


def remote(src, dst, send_sem, recv_sem, device):
    return pltpu.make_async_remote_copy(
        src_ref=src,
        dst_ref=dst,
        send_sem=send_sem,
        recv_sem=recv_sem,
        device_id=device,
        device_id_type=MESH,
    )


def send(*args):
    copy = remote(*args)
    copy.start()
    return copy


def fetch(src, dst, sem):
    copy = pltpu.make_async_copy(src, dst, sem)
    copy.start()
    return copy


def others(axis, count):
    me = lax.axis_index(axis)
    return [lax.rem(me + k, count) for k in range(1, count)]


def flip(index):
    return index + 1 - 2 * lax.rem(index, 2)


def pack_edge(lane, part, shift):
    total = None
    for level in range(PAIR):
        moved = pltpu.roll(part(level), (2 * HALF * level + shift) % LANES, 1)
        total = moved if total is None else jnp.where(jnp.right_shift(lane, 3) == level, moved, total)
    return total


def unpack_edge(lane, packed, level):
    moved = pltpu.roll(packed, (LANES - 2 * HALF * level) % LANES, 1)
    return jnp.where(lane < 2 * HALF, moved, 0.0)


def front_kernel(
    levs,
    count,
    scale,
    ext_hbm,
    owner_hbm,
    control_hbm,
    members_hbm,
    kern_hbm,
    col_hbm,
    inn_hbm,
    w_hbm,
    cnt_hbm,
    kron_hbm,
    hi_hbm,
    lo_hbm,
    misfit_ref,
    mixed_all,
    edge_all,
    ext_s,
    owner_s,
    control_v,
    members_v,
    kern_v,
    col_v,
    inn_v,
    w_v,
    cnt_v,
    kron_v,
    hi_v,
    lo_v,
    ctrl_all,
    ctrl_edge,
    mixed_v,
    mixed_own,
    edge_own,
    edge_out,
    edge_in,
    vert_v,
    field_all,
    field_v,
    part_v,
    chip_v,
    near_in,
    cross_out,
    cross_in,
    local_sem,
    ctl_sem,
    c_far,
    c_near,
    c_on,
    h_sem,
    f_sem,
    n_sem,
    x_sem,
    y_sem,
    m_far,
    m_near,
    m_on,
    m_loc,
):
    levels, members, width = control_v.shape
    tiles = width // LANES
    halves = members // PAIR
    blocks = col_v.shape[0]
    rows = blocks // levs
    lev, me = lax.axis_index("lev"), lax.axis_index("horiz")
    near, far = flip(lev), lax.rem(lev + 2, levs)
    across = flip(far)
    right, left = lax.rem(me + 1, count), lax.rem(me + count - 1, count)
    own = pl.ds(pl.multiple_of(lev * levels, levels), levels)
    afar = pl.ds(pl.multiple_of(far * levels, levels), levels)
    side, part = lax.rem(lev, 2), rows // 2

    tile_cols = [pl.ds(t * LANES, LANES) for t in range(tiles)]
    half_rows = [pl.ds(half * PAIR, PAIR) for half in range(halves)]
    all_here = greet(
        [{"lev": side} for side in others("lev", levs)]
        + [{"horiz": peer} for peer in others("horiz", count)]
    )
    ctl = [
        fetch(control_hbm.at[:, :, c], control_v.at[:, :, c], ctl_sem.at[t])
        for t, c in enumerate(tile_cols)
    ]
    away, beside, onward = {}, {}, {}

    def share(t, block):
        away[t] = send(block, block, c_far.at[0, t], c_far.at[1, t], {"lev": far})
        beside[t] = send(block, block, c_near.at[0, t], c_near.at[1, t], {"lev": near})

    def pass_on(t, block):
        away[t].wait_recv()
        onward[t] = send(block, block, c_on.at[0, t], c_on.at[1, t], {"lev": near})

    def share_tile(t):
        for half in range(halves):
            ctrl_all[half, own, :, tile_cols[t]] = control_v[:, half_rows[half], tile_cols[t]].astype(BF)
        share(t, ctrl_all.at[:, own, :, tile_cols[t]])

    lane = lax.broadcasted_iota(jnp.int32, (PAIR, LANES), 1)
    low_lane = jnp.bitwise_and(lane, 2 * HALF - 1)
    after = HALF * jnp.where(me < count - 1, 1, 0)
    before = HALF * jnp.where(me > 0, 1, 0)

    def send_edges(which, source):
        first, last = source.at[:, :, tile_cols[0]], source.at[:, :, tile_cols[tiles - 1]]
        copies = []
        for side, (view, shift, peer) in enumerate(((first, 0, left), (last, 2 * HALF, right))):
            for half in range(halves):
                packed = pack_edge(lane, lambda level: view[level, half_rows[half], :], shift)
                edge_out[which, side, half] = packed.astype(BF)
            copies.append(
                send(
                    edge_out.at[which, side],
                    edge_in.at[which, side],
                    h_sem.at[0, which, side],
                    h_sem.at[1, which, side],
                    {"horiz": peer},
                )
            )
        return copies

    def merged_edge(which, half):
        edge = jnp.where(low_lane < after, edge_in[which, 0, half].astype(F32), 0.0)
        return jnp.where(
            (low_lane >= HALF) & (low_lane < HALF + before),
            edge_in[which, 1, half].astype(F32),
            edge,
        ).astype(BF)

    early = tiles // 2
    all_here()
    ctl[0].wait()
    share_tile(0)
    local = [
        fetch(src, dst, local_sem.at[k])
        for k, (src, dst) in enumerate(
            [
                (ext_hbm, ext_s),
                (members_hbm, members_v),
                (
                    kron_hbm.at[pl.ds(pl.multiple_of(lev * levels * PAIR, levels * PAIR), levels * PAIR)],
                    kron_v,
                ),
                (hi_hbm, hi_v),
                (lo_hbm, lo_v),
                (owner_hbm, owner_s),
                (kern_hbm, kern_v),
                (col_hbm, col_v),
                (inn_hbm, inn_v),
                (w_hbm, w_v),
                (cnt_hbm, cnt_v),
            ]
        )
    ]
    for t in range(1, tiles):
        ctl[t].wait()
        if t < early:
            share_tile(t)
    control_edges = send_edges(0, control_v)

    local[0].wait()
    local[1].wait()
    for t in range(tiles):
        total = ext_s[0] * members_v[:, 0, :, tile_cols[t]].astype(F32)
        for species in range(1, members_v.shape[1]):
            total = total + ext_s[species] * members_v[:, species, :, tile_cols[t]].astype(F32)
        mixed_v[:, :, tile_cols[t]] = total
        for half in range(halves):
            mixed_own[half, :, :, tile_cols[t]] = total[:, half * PAIR : (half + 1) * PAIR].astype(BF)
    mixed_edges = send_edges(1, mixed_v)

    for copy in control_edges:
        copy.wait_recv()
    for half in range(halves):
        ctrl_edge[lev, half] = merged_edge(0, half)
    share(tiles, ctrl_edge.at[lev])
    for t in range(early, tiles):
        share_tile(t)
    for copy in mixed_edges:
        copy.wait_recv()
    for half in range(halves):
        edge_own[half] = merged_edge(1, half)

    for k in range(2, 5):
        local[k].wait()

    def raise_tile(t):
        pass_on(t, ctrl_all.at[:, afar, :, tile_cols[t]])
        if t == tiles - 1:
            start_mixed()
        beside[t].wait_recv()
        onward[t].wait_recv()
        for half in range(halves):
            x = ctrl_all[half, :, :, tile_cols[t]].reshape(LEV * PAIR, LANES)
            vert_v[half, :, tile_cols[t]] = dot(kron_v[...], x).astype(BF)

    def raise_edge():
        pass_on(tiles, ctrl_edge.at[far])
        beside[tiles].wait_recv()
        onward[tiles].wait_recv()
        for half in range(halves):
            x = []
            for slab in range(levs):
                packed = ctrl_edge[slab, half].astype(F32)
                x += [unpack_edge(lane, packed, level).astype(BF) for level in range(levels)]
            x = jnp.concatenate(x, axis=0)
            vert_v[half, :, pl.ds(width, LANES)] = dot(kron_v[...], x).astype(BF)

    m_away, m_beside, m_onward, m_kept = [], [], [], []

    def start_mixed():
        parts = [(mixed_own.at[half], mixed_all.at[half, own]) for half in range(halves)]
        parts.append((edge_own, edge_all.at[lev]))
        for k, (block, place) in enumerate(parts):
            m_away.append(send(block, place, m_far.at[0, k], m_far.at[1, k], {"lev": far}))
            m_beside.append(send(block, place, m_near.at[0, k], m_near.at[1, k], {"lev": near}))
            m_kept.append(fetch(block, place, m_loc.at[k]))

    f_copies = {}

    def make_field(t):
        spans = [pl.ds(max(t - 1, 0) * LANES, (min(t + 2, tiles) - max(t - 1, 0)) * LANES)]
        if t in (0, tiles - 1):
            spans.append(pl.ds(width, LANES))
        total = None
        for half in range(halves):
            inc = None
            for cols in spans:
                v = vert_v[half, :, cols]
                term = dot(v, hi_v[cols, tile_cols[t]]) + dot(v, lo_v[cols, tile_cols[t]])
                inc = term if inc is None else inc + term
            inc = inc.reshape(levels, PAIR, LANES)
            term = jnp.sum(mixed_v[:, half_rows[half], tile_cols[t]] * inc, axis=1)
            total = term if total is None else total + term
        field_all[me, t] = (total * scale).astype(BF)

    def send_field(group):
        block = field_all.at[me, pl.ds(group[0], len(group))]
        f_copies[group] = [
            send(
                block, block, f_sem.at[0, group[0], k], f_sem.at[1, group[0], k], {"horiz": peer}
            )
            for k, peer in enumerate(others("horiz", count))
        ]

    def take_field(group):
        for copy in f_copies[group]:
            copy.wait_recv()
        for t in group:
            for h in range(count):
                field_v[h, t] = field_all[h, t].astype(F32)

    def forward(peer, chosen, first):
        start = pl.multiple_of(peer * rows, rows)

        def step(group, carry):
            base = pl.multiple_of(start + group * GROUP, GROUP)
            cols = col_v[pl.ds(base, GROUP), :]
            out = []
            for i in range(GROUP):
                owner = owner_s[base + i]
                col = jnp.broadcast_to(cols[i : i + 1, :], (levels, LANES))
                low = jnp.bitwise_and(col, LANES - 1)
                high = jnp.right_shift(col, 7)
                picked = 0.0
                for tile in chosen:
                    value = jnp.take_along_axis(field_v[owner, tile], low, axis=1)
                    picked = jnp.where(high == tile, value, picked)
                prod = picked * kern_v[base + i].astype(F32)
                out.append(jnp.sum(prod, axis=0, keepdims=True))
            value = jnp.concatenate(out, axis=0)
            if not first:
                value = value + part_v[pl.ds(base, GROUP), :]
            part_v[pl.ds(base, GROUP), :] = value
            return carry

        lax.fori_loop(0, rows // GROUP, step, 0)

    def forward_all(chosen, first):
        lax.fori_loop(0, levs, lambda k, carry: (forward(k, chosen, first), carry)[1], 0)

    one, two = tuple(range(early)), tuple(range(early, tiles))
    raise_tile(0)
    raise_edge()
    raise_tile(1)
    make_field(0)
    for k in range(5, 8):
        local[k].wait()
    for t in range(2, tiles):
        raise_tile(t)
        make_field(t - 1)
        if t == early:
            send_field(one)
    make_field(tiles - 1)
    send_field(two)
    take_field(one)
    forward_all(one, True)
    take_field(two)

    def span(k):
        return pl.ds(pl.multiple_of(k * rows, rows), rows)

    def near_copy(k):
        return remote(
            part_v.at[span(k)], near_in.at[k], n_sem.at[0, k], n_sem.at[1, k], {"lev": near}
        )

    def cross_copy(k):
        return remote(
            cross_out.at[k], cross_in.at[k, side], x_sem.at[0, k], x_sem.at[1, k], {"lev": far}
        )

    def hand_copy(k):
        block = cross_in.at[k, side]
        return remote(block, block, y_sem.at[0, k], y_sem.at[1, k], {"lev": near})

    def sum_chip(k):
        near_copy(k).wait_recv()
        chip_v[span(k), :] = part_v[span(k), :] + near_in[k]
        own_part = pl.ds(pl.multiple_of(k * rows + side * part, part), part)
        cross_out[k] = chip_v[own_part, :].astype(BF)
        cross_copy(k).start()

    def hand_on(k):
        cross_copy(k).wait_recv()
        hand_copy(k).start()

    def one_part(k, carry):
        forward(k, two, False)
        near_copy(k).start()

        @pl.when(k >= 1)
        def _():
            sum_chip(k - 1)

        @pl.when(k >= 3)
        def _():
            hand_on(k - 3)

        return carry

    lax.fori_loop(0, levs, one_part, 0)
    sum_chip(levs - 1)

    for k in range(8, 11):
        local[k].wait()

    lane_row = lax.broadcasted_iota(jnp.int32, (rows, LANES), 1).astype(F32)
    for k in range(levs):
        if k >= levs - 3:
            hand_on(k)
    places = [mixed_all.at[half, afar] for half in range(halves)] + [edge_all.at[far]]
    for k, place in enumerate(places):
        m_away[k].wait_recv()
        m_onward.append(send(place, place, m_on.at[0, k], m_on.at[1, k], {"lev": near}))
    for k in range(levs):
        hand_copy(k).wait_recv()
        other = jnp.concatenate([cross_in[k, 0], cross_in[k, 1]], axis=0).astype(F32)
        evolved = chip_v[pl.ds(k * rows, rows), :] + other
        block = pl.ds(k * rows, rows)
        misfit = w_v[block, :].astype(F32) * (evolved - inn_v[block, :].astype(F32)) * scale
        counts = jnp.broadcast_to(cnt_v[pl.ds(k, 1), :].astype(F32), (LANES, LANES))
        live = lane_row < jnp.transpose(counts)
        misfit_ref[block, :] = jnp.where(live, misfit, 0.0).astype(BF)

    for k in range(levs):
        near_copy(k).wait_send()
        cross_copy(k).wait_send()
        hand_copy(k).wait_send()
    for copies in f_copies.values():
        for copy in copies:
            copy.wait_send()
    for group in (away, beside, onward):
        for copy in group.values():
            copy.wait_send()
    for copy in control_edges + mixed_edges + m_away:
        copy.wait_send()
    for copy in m_beside + m_onward + m_kept:
        copy.wait()


def adjoint_kernel(owner_ref, kern_ref, col_ref, mis_ref, out_ref, acc):
    blocks = col_ref.shape[0]
    levels = kern_ref.shape[1]
    count = acc.shape[0]
    tiles = acc.shape[2] // levels
    acc[...] = jnp.zeros_like(acc)
    lane_row = lax.broadcasted_iota(jnp.int32, (LANES, LANES), 0).astype(F32).astype(BF)
    one, zero = jnp.ones((), BF), jnp.zeros((), BF)

    def step(group, carry):
        base = pl.multiple_of(group * MANY, MANY)
        cols = col_ref[pl.ds(base, MANY), :]
        low = jnp.bitwise_and(cols, LANES - 1).astype(F32)
        high = jnp.right_shift(cols, 7)
        misfit = mis_ref[pl.ds(base, MANY), :].astype(F32)
        parts = [jnp.where(high == tile, misfit, 0.0) for tile in range(tiles)]
        for i in range(MANY):
            owner = owner_ref[base + i]
            kern = kern_ref[base + i]
            rows = jnp.concatenate(
                [
                    kern * jnp.broadcast_to(part[i : i + 1, :], (levels, LANES)).astype(BF)
                    for part in parts
                ],
                axis=0,
            )
            row = jnp.broadcast_to(low[i : i + 1, :], (LANES, LANES)).astype(BF)
            hot = jnp.where(lane_row == row, one, zero)
            acc[owner] += lax.dot_general(
                hot, rows, (((1,), (1,)), ((), ())), preferred_element_type=F32
            )
        return carry

    lax.fori_loop(0, blocks // MANY, step, 0)

    lane = lax.broadcasted_iota(jnp.int32, (levels, LANES), 1)
    sums = [jnp.transpose(acc[h]) for h in range(count)]
    for h in range(count):
        out_ref[h, pl.ds(0, tiles * levels)] = sums[h].astype(BF)
        edge = jnp.zeros((levels, LANES), F32)
        if h < count - 1:
            edge = jnp.where(lane < HALF, sums[h + 1][:levels], edge)
        if h > 0:
            moved = pltpu.roll(sums[h - 1][(tiles - 1) * levels :], 2 * HALF, 1)
            edge = jnp.where((lane >= HALF) & (lane < 2 * HALF), moved, edge)
        out_ref[h, pl.ds(tiles * levels, levels)] = edge.astype(BF)


def back_kernel(
    count,
    levs,
    x_ref,
    mixed_hbm,
    edge_hbm,
    kron_hbm,
    out_ref,
    mixed_v,
    edge_v,
    kron_v,
    fg_v,
    slots,
    r_sem,
    a_sem,
    local_sem,
):
    halves, size, full = out_ref.shape
    levels = size // PAIR
    tiles = full // LANES
    early = (tiles - 1) // 2
    groups = [range(early), range(early, tiles)]
    rows = [pl.ds(group[0] * levels, len(group) * levels) for group in groups]
    me, lev = lax.axis_index("horiz"), lax.axis_index("lev")
    near, far = flip(lev), lax.rem(lev + 2, levs)
    sides = [near, far, flip(far)]
    peers = others("horiz", count)
    greet([{"horiz": peer} for peer in peers] + [{"lev": side} for side in sides])()
    reduce = [
        [
            send(
                x_ref.at[peer, part],
                slots.at[k, part],
                r_sem.at[0, g, k],
                r_sem.at[1, g, k],
                {"horiz": peer},
            )
            for k, peer in enumerate(peers)
        ]
        for g, part in enumerate(rows)
    ]
    at = pl.multiple_of(lev * size, size)
    local = [
        fetch(mixed_hbm, mixed_v, local_sem.at[0]),
        fetch(edge_hbm, edge_v, local_sem.at[1]),
        fetch(kron_hbm.at[pl.ds(at, size)], kron_v, local_sem.at[2]),
    ]
    lane = lax.broadcasted_iota(jnp.int32, (PAIR, LANES), 1)

    def total_up(g):
        part = rows[g]
        total = x_ref[me, part].astype(F32)
        for k, copy in enumerate(reduce[g]):
            copy.wait_recv()
            total = total + slots[k, part].astype(F32)
        fg_v[lev, part] = total
        block = fg_v.at[lev, part]
        return [
            send(block, block, a_sem.at[0, g, k], a_sem.at[1, g, k], {"lev": side})
            for k, side in enumerate(sides)
        ]

    def slab(index, g, first):
        start = pl.multiple_of(index * levels, levels)
        begin = pl.multiple_of(index * size, size)
        group = groups[g]
        span = pl.ds(group[0] * LANES, len(group) * LANES)
        for half in range(halves):
            columns = []
            for t in group:
                fg = fg_v[index, pl.ds(t * levels, levels), :]
                if t < tiles - 1:
                    m = mixed_v[half, pl.ds(start, levels), :, pl.ds(t * LANES, LANES)]
                    grad = (m.astype(F32) * fg[:, None, :]).astype(BF).reshape(size, LANES)
                else:
                    packed = edge_v[index, half].astype(F32)
                    grad = jnp.concatenate(
                        [
                            (unpack_edge(lane, packed, level) * fg[level : level + 1, :]).astype(BF)
                            for level in range(levels)
                        ],
                        axis=0,
                    )
                columns.append(grad)
            term = dot(kron_v[:, pl.ds(begin, size)], jnp.concatenate(columns, axis=1))
            out_ref[half, :, span] = term if first else out_ref[half, :, span] + term

    spread = [total_up(0)]
    for copy in local:
        copy.wait()
    slab(lev, 0, True)
    spread.append(total_up(1))
    slab(lev, 1, True)
    for g in range(2):
        for k, side in enumerate(sides):
            spread[g][k].wait_recv()
            slab(side, g, False)
    for copies in reduce + spread:
        for copy in copies:
            copy.wait_send()


def final_kernel(levels_ref, hi_ref, lo_ref, control_ref, out_hbm, out_v, sem):
    levels, members, width = control_ref.shape
    copies = []
    for half in range(members // PAIR):
        part = pl.ds(half * PAIR, PAIR)
        mixed_levels = levels_ref[half]
        high = mixed_levels.astype(BF)
        low = (mixed_levels - high.astype(F32)).astype(BF)
        total = dot(high, hi_ref[...]) + dot(high, lo_ref[...]) + dot(low, hi_ref[...])
        out_v[half] = control_ref[:, part, :] + total.reshape(levels, PAIR, width)
        copies.append(fetch(out_v.at[half], out_hbm.at[:, part, :], sem.at[half]))
    for copy in copies:
        copy.wait()


def vmem(count):
    return [pl.BlockSpec(memory_space=pltpu.VMEM)] * count


def smem(count):
    return [pl.BlockSpec(memory_space=pltpu.SMEM)] * count


def hbm(count):
    return [pl.BlockSpec(memory_space=pltpu.HBM)] * count


def pairs(*size):
    return pltpu.SemaphoreType.DMA((2,) + size)


def body(
    control,
    members,
    extinction,
    kernels,
    innovation,
    obs_weight,
    owners,
    pixel_columns,
    pixel_counts,
):
    levels, mem_count, width = control.shape
    blocks, _, pixels = kernels.shape
    count, levs = lax.axis_size("horiz"), lax.axis_size("lev")
    tiles = width // LANES
    halves = mem_count // PAIR
    rows = blocks // levs
    full = width + LANES
    kron_all = spread_levels(level_matrix())
    high, low = tap_matrix(width)
    hi, lo = jnp.asarray(high), jnp.asarray(low)
    scale = 1.0 / math.sqrt(mem_count)
    owner_ids = owners[:, 0]

    misfit, mixed_all, edge_all = pl.pallas_call(
        functools.partial(front_kernel, levs, count, scale),
        out_shape=[
            jax.ShapeDtypeStruct((blocks, pixels), BF),
            jax.ShapeDtypeStruct((halves, levs * levels, PAIR, width), BF),
            jax.ShapeDtypeStruct((levs, halves, PAIR, LANES), BF),
        ],
        in_specs=hbm(12),
        out_specs=vmem(1) + hbm(2),
        scratch_shapes=[
            pltpu.SMEM(extinction.shape, F32),
            pltpu.SMEM(owner_ids.shape, jnp.int32),
            pltpu.VMEM(control.shape, F32),
            pltpu.VMEM(members.shape, BF),
            pltpu.VMEM(kernels.shape, BF),
            pltpu.VMEM(pixel_columns.shape, jnp.int32),
            pltpu.VMEM((blocks, pixels), BF),
            pltpu.VMEM((blocks, pixels), BF),
            pltpu.VMEM((levs, rows), jnp.int32),
            pltpu.VMEM((levels * PAIR, LEV * PAIR), BF),
            pltpu.VMEM((full, width), BF),
            pltpu.VMEM((full, width), BF),
            pltpu.VMEM((halves, levs * levels, PAIR, width), BF),
            pltpu.VMEM((levs, halves, PAIR, LANES), BF),
            pltpu.VMEM((levels, mem_count, width), F32),
            pltpu.VMEM((halves, levels, PAIR, width), BF),
            pltpu.VMEM((halves, PAIR, LANES), BF),
            pltpu.VMEM((2, 2, halves, PAIR, LANES), BF),
            pltpu.VMEM((2, 2, halves, PAIR, LANES), BF),
            pltpu.VMEM((halves, levels * PAIR, full), BF),
            pltpu.VMEM((count, tiles, levels, LANES), BF),
            pltpu.VMEM((count, tiles, levels, LANES), F32),
            pltpu.VMEM((blocks, pixels), F32),
            pltpu.VMEM((blocks, pixels), F32),
            pltpu.VMEM((levs, rows, pixels), F32),
            pltpu.VMEM((levs, rows // 2, pixels), BF),
            pltpu.VMEM((levs, 2, rows // 2, pixels), BF),
            pltpu.SemaphoreType.DMA((11,)),
            pltpu.SemaphoreType.DMA((tiles,)),
            pairs(tiles + 1),
            pairs(tiles + 1),
            pairs(tiles + 1),
            pairs(2, 2),
            pairs(tiles, count - 1),
            pairs(levs),
            pairs(levs),
            pairs(levs),
            pairs(halves + 1),
            pairs(halves + 1),
            pairs(halves + 1),
            pltpu.SemaphoreType.DMA((halves + 1,)),
        ],
        compiler_params=pltpu.CompilerParams(
            vmem_limit_bytes=58 * MIB, collective_id=0, has_side_effects=True
        ),
    )(
        extinction,
        owner_ids,
        control,
        members,
        kernels,
        pixel_columns,
        innovation,
        obs_weight,
        pixel_counts.reshape(levs, rows),
        kron_all,
        hi,
        lo,
    )

    partial = pl.pallas_call(
        adjoint_kernel,
        out_shape=jax.ShapeDtypeStruct((count, (tiles + 1) * levels, LANES), BF),
        in_specs=smem(1) + vmem(3),
        out_specs=pl.BlockSpec(memory_space=pltpu.VMEM),
        scratch_shapes=[pltpu.VMEM((count, LANES, tiles * levels), F32)],
        compiler_params=pltpu.CompilerParams(vmem_limit_bytes=32 * MIB),
    )(owner_ids, kernels, pixel_columns, misfit)

    levels_mixed = pl.pallas_call(
        functools.partial(back_kernel, count, levs),
        out_shape=jax.ShapeDtypeStruct((halves, levels * PAIR, full), F32),
        in_specs=vmem(1) + hbm(3),
        out_specs=pl.BlockSpec(memory_space=pltpu.VMEM),
        scratch_shapes=[
            pltpu.VMEM(mixed_all.shape, BF),
            pltpu.VMEM(edge_all.shape, BF),
            pltpu.VMEM((levels * PAIR, LEV * PAIR), BF),
            pltpu.VMEM((levs, (tiles + 1) * levels, LANES), F32),
            pltpu.VMEM((count - 1, (tiles + 1) * levels, LANES), BF),
            pairs(2, count - 1),
            pairs(2, levs - 1),
            pltpu.SemaphoreType.DMA((3,)),
        ],
        compiler_params=pltpu.CompilerParams(
            vmem_limit_bytes=50 * MIB, collective_id=1, has_side_effects=True
        ),
    )(partial, mixed_all, edge_all, kron_all)

    return pl.pallas_call(
        final_kernel,
        out_shape=jax.ShapeDtypeStruct(control.shape, F32),
        in_specs=vmem(4),
        out_specs=pl.BlockSpec(memory_space=pltpu.HBM),
        scratch_shapes=[
            pltpu.VMEM((halves, levels, PAIR, width), F32),
            pltpu.SemaphoreType.DMA((halves,)),
        ],
        compiler_params=pltpu.CompilerParams(vmem_limit_bytes=32 * MIB),
    )(levels_mixed, hi, lo, control)


def solution(mesh):
    placed = (
        P("lev", None, "horiz"),
        P("lev", None, None, "horiz"),
        P(),
        P("horiz", "lev", None),
        P("horiz", None),
        P("horiz", None),
        P("horiz", None),
        P("horiz", None),
        P("horiz"),
    )
    return jax.shard_map(
        body, mesh=mesh, in_specs=placed, out_specs=P("lev", None, "horiz"), check_vma=False
    )
```

time: 62.1 us -> 61 us (0.982)
  other arithmetic: 1.21 us -> 0 us
    pallas_call x0 -> x1, Pallas kernels: none -> 2.19 us  [body(): pl.pallas_call(final_kernel, out_shape=jax.ShapeDtypeStruct(control.shape...]
    add x1 -> x0, other arithmetic: 1.21 us -> none  [body(): return control + delta]
    pallas_call x1, Pallas kernels: 12.1 us -> 11.1 us  [body(): pl.pallas_call(functools.partial(back_kernel, count, levs), out_shape=jax...]
where the time goes in v3:
time: 61 us; the launch traced here: 60.9 us
  Pallas kernels  59.7 us (98%)
  local copies, waits for them, and re-layouts  1.08 us (2%)
    pallas_call x1, Pallas kernels, body(): pl.pallas_call(functools.partial(front_kernel, levs, count, scale), out_s...  40.4 us
    pallas_call x1, Pallas kernels, body(): pl.pallas_call(functools.partial(back_kernel, count, levs), out_shape=jax...  11.1 us
    pallas_call x1, Pallas kernels, body(): pl.pallas_call(adjoint_kernel, out_shape=jax.ShapeDtypeStruct((count, (ti...  6.06 us
    pallas_call x1, Pallas kernels, body(): pl.pallas_call(final_kernel, out_shape=jax.ShapeDtypeStruct(control.shape...  2.19 us

profile of v3, /device:TPU:0, one launch (start us, length us, event | category | flops | bytes accessed | tf_op | source)
XLA Modules:
  0.0 60.9 jit_solution(14690992816538674960)
XLA Ops:
  0.0 0.0 copy-start
  0.0 0.0 copy-start.5
  0.0 0.0 copy-start.8
  0.0 40.4 %shard_map.118 = (bf16[512,128]{1,0:T(8,128)(2,1)}, bf16[2,64,16,512]{3,2,1,0:T(8,128)(2,1)}, bf16[4,2,16,128]{3,2,1,0:T(8,128)(2,1)}) custom-call(f32[4]{0:T(128)} %ext_hbm.1, s32[512]{0:T(512)} %bitcast.2, f32[16,32,512]{2,1,0:T(8,128)} %control_ref.1, bf16[16,4,32,512]{3,2,1,0:T(8,128)(2,1)} %members_hbm.1, bf16[512,16,128]{2,1,0:T(8,128)(2,1)} %kern_ref.1, ...), custom_call_target="tpu_custom_call" | custom-call | tf_op jit(solution)/shard_map/pallas_call | solution.py:699
  40.4 0.0 copy-start.4
  40.4 0.0 copy-done
  40.4 0.0 copy-done.5
  40.4 0.0 copy-done.8
  40.4 0.0 copy-start.6
  40.4 1.0 %copy-done.6 = bf16[512,128]{1,0:T(8,128)(2,1)S(1)} copy-done((bf16[512,128]{1,0:T(8,128)(2,1)S(1)}, bf16[512,128]{1,0:T(8,128)(2,1)}, u32[]{:S(2)}) %copy-start.6) | copy-done | bytes 131096
  41.5 0.0 copy-start.7
  41.5 6.1 %shard_map.119.x_ref = bf16[8,80,128]{2,1,0:T(8,128)(2,1)S(1)} custom-call(s32[512]{0:T(512)S(1)} %bitcast.3, bf16[512,16,128]{2,1,0:T(8,128)(2,1)S(1)} %copy-done, s32[512,128]{1,0:T(8,128)S(1)} %copy-done.5, bf16[512,128]{1,0:T(8,128)(2,1)S(1)} %copy-done.6), custom_call_target="tpu_custom_call" | custom-call | tf_op jit(solution)/shard_map/pallas_call | solution.py:769
  47.5 0.0 copy-done.4
  47.5 0.0 copy-done.7
  47.5 0.0 copy-start.1
  47.5 0.0 copy-start.2
  47.6 0.0 copy-start.3
  47.6 11.1 %shard_map.120.levels_ref = f32[2,256,640]{2,1,0:T(8,128)S(1)} custom-call(bf16[8,80,128]{2,1,0:T(8,128)(2,1)S(1)} %shard_map.119.x_ref, bf16[2,64,16,512]{3,2,1,0:T(8,128)(2,1)S(1)} %copy-done.4, bf16[4,2,16,128]{3,2,1,0:T(8,128)(2,1)S(1)} %copy-done.7, bf16[1024,1024]{1,0:T(8,128)(2,1)} %constant.6.clone.kron_hbm), custom_call_target="tpu_custom_call" | custom-call | tf_op jit(solution)/shard_map/pallas_call | solution.py:778
  58.6 0.0 copy-done.1
  58.7 0.0 copy-done.2
  58.7 0.0 copy-done.3
  58.7 2.2 %shard_map.121 = f32[16,32,512]{2,1,0:T(8,128)} custom-call(f32[2,256,640]{2,1,0:T(8,128)S(1)} %shard_map.120.levels_ref, bf16[640,512]{1,0:T(8,128)(2,1)S(1)} %copy-done.3, bf16[640,512]{1,0:T(8,128)(2,1)S(1)} %copy-done.2, f32[16,32,512]{2,1,0:T(8,128)S(1)} %copy-done.1), custom_call_target="tpu_custom_call" | custom-call | tf_op jit(solution)/shard_map/pallas_call | solution.py:798
Async XLA Ops:
  0.0 40.4 %copy-start = (bf16[512,16,128]{2,1,0:T(8,128)(2,1)S(1)}, bf16[512,16,128]{2,1,0:T(8,128)(2,1)}, u32[]{:S(2)}) copy-start(bf16[512,16,128]{2,1,0:T(8,128)(2,1)} %kern_ref.1) | copy-start | bytes 6291460
  0.0 40.4 %copy-start.5 = (s32[512,128]{1,0:T(8,128)S(1)}, s32[512,128]{1,0:T(8,128)}, u32[]{:S(2)}) copy-start(s32[512,128]{1,0:T(8,128)} %col_ref.1) | copy-start | bytes 786436
  0.0 40.4 %copy-start.8 = (s32[512,1]{0,1:T(1,128)S(1)}, s32[512,1]{0,1:T(1,128)}, u32[]{:S(2)}) copy-start(s32[512,1]{0,1:T(1,128)} %param.18) | copy-start | bytes 6148
  40.4 7.1 %copy-start.4 = (bf16[2,64,16,512]{3,2,1,0:T(8,128)(2,1)S(1)}, bf16[2,64,16,512]{3,2,1,0:T(8,128)(2,1)}, u32[]{:S(2)}) copy-start(bf16[2,64,16,512]{3,2,1,0:T(8,128)(2,1)} %get-tuple-element.9.mixed_hbm) | copy-start | bytes 6291460
  40.4 1.0 %copy-start.6 = (bf16[512,128]{1,0:T(8,128)(2,1)S(1)}, bf16[512,128]{1,0:T(8,128)(2,1)}, u32[]{:S(2)}) copy-start(bf16[512,128]{1,0:T(8,128)(2,1)} %get-tuple-element.8.mis_ref) | copy-start | bytes 393220
  41.5 6.1 %copy-start.7 = (bf16[4,2,16,128]{3,2,1,0:T(8,128)(2,1)S(1)}, bf16[4,2,16,128]{3,2,1,0:T(8,128)(2,1)}, u32[]{:S(2)}) copy-start(bf16[4,2,16,128]{3,2,1,0:T(8,128)(2,1)} %get-tuple-element.10.edge_hbm) | copy-start | bytes 98308
  47.5 11.1 %copy-start.1 = (f32[16,32,512]{2,1,0:T(8,128)S(1)}, f32[16,32,512]{2,1,0:T(8,128)}, u32[]{:S(2)}) copy-start(f32[16,32,512]{2,1,0:T(8,128)} %control_ref.1) | copy-start | bytes 3145732
  47.5 11.1 %copy-start.2 = (bf16[640,512]{1,0:T(8,128)(2,1)S(1)}, bf16[640,512]{1,0:T(8,128)(2,1)}, u32[]{:S(2)}) copy-start(bf16[640,512]{1,0:T(8,128)(2,1)} %constant.8.clone.lo_hbm.lo_ref) | copy-start | bytes 1966084
  47.6 11.1 %copy-start.3 = (bf16[640,512]{1,0:T(8,128)(2,1)S(1)}, bf16[640,512]{1,0:T(8,128)(2,1)}, u32[]{:S(2)}) copy-start(bf16[640,512]{1,0:T(8,128)(2,1)} %constant.7.clone.hi_hbm.hi_ref) | copy-start | bytes 1966084

commit v4 on v3

--- a/solution.py
+++ b/solution.py
@@ -127,6 +127,8 @@
     lo_hbm,
     misfit_ref,
     mixed_all,
+    mixed_low,
+    mixed_rest,
     edge_all,
     ext_s,
     owner_s,
@@ -321,7 +323,11 @@
     m_away, m_beside, m_onward, m_kept = [], [], [], []
 
     def start_mixed():
-        parts = [(mixed_own.at[half], mixed_all.at[half, own]) for half in range(halves)]
+        cut = levels // 2
+        rest = mixed_own.at[halves - 1, pl.ds(cut, cut)]
+        m_kept.append(fetch(rest, mixed_rest, m_loc.at[halves + 1]))
+        parts = [(mixed_own.at[half], mixed_all.at[half, own]) for half in range(halves - 1)]
+        parts.append((mixed_own.at[halves - 1, pl.ds(0, cut)], mixed_low.at[lev]))
         parts.append((edge_own, edge_all.at[lev]))
         for k, (block, place) in enumerate(parts):
             m_away.append(send(block, place, m_far.at[0, k], m_far.at[1, k], {"lev": far}))
@@ -461,7 +467,8 @@
     for k in range(levs):
         if k >= levs - 3:
             hand_on(k)
-    places = [mixed_all.at[half, afar] for half in range(halves)] + [edge_all.at[far]]
+    places = [mixed_all.at[half, afar] for half in range(halves - 1)]
+    places += [mixed_low.at[far], edge_all.at[far]]
     for k, place in enumerate(places):
         m_away[k].wait_recv()
         m_onward.append(send(place, place, m_on.at[0, k], m_on.at[1, k], {"lev": near}))
@@ -544,16 +551,21 @@
     levs,
     x_ref,
     mixed_hbm,
+    low_hbm,
+    rest_hbm,
     edge_hbm,
     kron_hbm,
     out_ref,
     mixed_v,
+    low_v,
+    rest_v,
     edge_v,
     kron_v,
     fg_v,
     slots,
     r_sem,
     a_sem,
+    m_sem,
     local_sem,
 ):
     halves, size, full = out_ref.shape
@@ -580,11 +592,16 @@
         ]
         for g, part in enumerate(rows)
     ]
+    place = rest_v.at[lev]
+    m_away = send(rest_hbm, place, m_sem.at[0, 0], m_sem.at[1, 0], {"lev": far})
+    m_beside = send(rest_hbm, place, m_sem.at[0, 1], m_sem.at[1, 1], {"lev": near})
     at = pl.multiple_of(lev * size, size)
     local = [
         fetch(mixed_hbm, mixed_v, local_sem.at[0]),
         fetch(edge_hbm, edge_v, local_sem.at[1]),
         fetch(kron_hbm.at[pl.ds(at, size)], kron_v, local_sem.at[2]),
+        fetch(low_hbm, low_v, local_sem.at[3]),
+        fetch(rest_hbm, rest_v.at[lev], local_sem.at[4]),
     ]
     lane = lax.broadcasted_iota(jnp.int32, (PAIR, LANES), 1)
 
@@ -611,7 +628,13 @@
             for t in group:
                 fg = fg_v[index, pl.ds(t * levels, levels), :]
                 if t < tiles - 1:
-                    m = mixed_v[half, pl.ds(start, levels), :, pl.ds(t * LANES, LANES)]
+                    cols = pl.ds(t * LANES, LANES)
+                    if half < halves - 1:
+                        m = mixed_v[half, pl.ds(start, levels), :, cols]
+                    else:
+                        m = jnp.concatenate(
+                            [low_v[index, :, :, cols], rest_v[index, :, :, cols]], axis=0
+                        )
                     grad = (m.astype(F32) * fg[:, None, :]).astype(BF).reshape(size, LANES)
                 else:
                     packed = edge_v[index, half].astype(F32)
@@ -630,13 +653,18 @@
     for copy in local:
         copy.wait()
     slab(lev, 0, True)
+    m_away.wait_recv()
+    place = rest_v.at[far]
+    m_onward = send(place, place, m_sem.at[0, 2], m_sem.at[1, 2], {"lev": near})
     spread.append(total_up(1))
     slab(lev, 1, True)
     for g in range(2):
         for k, side in enumerate(sides):
             spread[g][k].wait_recv()
+            if g == 0 and k != 1:
+                (m_onward if k else m_beside).wait_recv()
             slab(side, g, False)
-    for copies in reduce + spread:
+    for copies in reduce + spread + [[m_away, m_beside, m_onward]]:
         for copy in copies:
             copy.wait_send()
 
@@ -696,15 +724,17 @@
     scale = 1.0 / math.sqrt(mem_count)
     owner_ids = owners[:, 0]
 
-    misfit, mixed_all, edge_all = pl.pallas_call(
+    misfit, mixed_all, mixed_low, mixed_rest, edge_all = pl.pallas_call(
         functools.partial(front_kernel, levs, count, scale),
         out_shape=[
             jax.ShapeDtypeStruct((blocks, pixels), BF),
-            jax.ShapeDtypeStruct((halves, levs * levels, PAIR, width), BF),
+            jax.ShapeDtypeStruct((halves - 1, levs * levels, PAIR, width), BF),
+            jax.ShapeDtypeStruct((levs, levels // 2, PAIR, width), BF),
+            jax.ShapeDtypeStruct((levels // 2, PAIR, width), BF),
             jax.ShapeDtypeStruct((levs, halves, PAIR, LANES), BF),
         ],
         in_specs=hbm(12),
-        out_specs=vmem(1) + hbm(2),
+        out_specs=vmem(1) + hbm(4),
         scratch_shapes=[
             pltpu.SMEM(extinction.shape, F32),
             pltpu.SMEM(owner_ids.shape, jnp.int32),
@@ -746,7 +776,7 @@
             pairs(halves + 1),
             pairs(halves + 1),
             pairs(halves + 1),
-            pltpu.SemaphoreType.DMA((halves + 1,)),
+            pltpu.SemaphoreType.DMA((halves + 2,)),
         ],
         compiler_params=pltpu.CompilerParams(
             vmem_limit_bytes=58 * MIB, collective_id=0, has_side_effects=True
@@ -778,22 +808,25 @@
     levels_mixed = pl.pallas_call(
         functools.partial(back_kernel, count, levs),
         out_shape=jax.ShapeDtypeStruct((halves, levels * PAIR, full), F32),
-        in_specs=vmem(1) + hbm(3),
+        in_specs=vmem(1) + hbm(5),
         out_specs=pl.BlockSpec(memory_space=pltpu.VMEM),
         scratch_shapes=[
             pltpu.VMEM(mixed_all.shape, BF),
+            pltpu.VMEM(mixed_low.shape, BF),
+            pltpu.VMEM(mixed_low.shape, BF),
             pltpu.VMEM(edge_all.shape, BF),
             pltpu.VMEM((levels * PAIR, LEV * PAIR), BF),
             pltpu.VMEM((levs, (tiles + 1) * levels, LANES), F32),
             pltpu.VMEM((count - 1, (tiles + 1) * levels, LANES), BF),
             pairs(2, count - 1),
             pairs(2, levs - 1),
-            pltpu.SemaphoreType.DMA((3,)),
+            pairs(3),
+            pltpu.SemaphoreType.DMA((5,)),
         ],
         compiler_params=pltpu.CompilerParams(
             vmem_limit_bytes=50 * MIB, collective_id=1, has_side_effects=True
         ),
-    )(partial, mixed_all, edge_all, kron_all)
+    )(partial, mixed_all, mixed_low, mixed_rest, edge_all, kron_all)
 
     return pl.pallas_call(
         final_kernel,

time: 61 us -> 60 us (0.984)
  Pallas kernels: 59.7 us -> 58.7 us
    pallas_call x1, Pallas kernels: 40.4 us -> 39.1 us  [body(): pl.pallas_call(functools.partial(front_kernel, levs, count, scale), out_s...]
where the time goes in v4:
time: 60 us; the launch traced here: 59.9 us
  Pallas kernels  58.7 us (98%)
  local copies, waits for them, and re-layouts  1.05 us (2%)
    pallas_call x1, Pallas kernels, body(): pl.pallas_call(functools.partial(front_kernel, levs, count, scale), out_s...  39.1 us
    pallas_call x1, Pallas kernels, body(): pl.pallas_call(functools.partial(back_kernel, count, levs), out_shape=jax...  11.3 us
    pallas_call x1, Pallas kernels, body(): pl.pallas_call(adjoint_kernel, out_shape=jax.ShapeDtypeStruct((count, (ti...  6.06 us
    pallas_call x1, Pallas kernels, body(): pl.pallas_call(final_kernel, out_shape=jax.ShapeDtypeStruct(control.shape...  2.19 us

profile of v4, /device:TPU:0, one launch (start us, length us, event | category | flops | bytes accessed | tf_op | source)
XLA Modules:
  0.0 59.9 jit_solution(876781044535124554)
XLA Ops:
  0.0 0.0 copy-start
  0.0 0.0 copy-start.4
  0.0 0.0 copy-start.10
  0.0 39.1 %shard_map.118 = (bf16[512,128]{1,0:T(8,128)(2,1)}, bf16[1,64,16,512]{3,2,1,0:T(8,128)(2,1)}, bf16[4,8,16,512]{3,2,1,0:T(8,128)(2,1)}, bf16[8,16,512]{2,1,0:T(8,128)(2,1)}, bf16[4,2,16,128]{3,2,1,0:T(8,128)(2,1)}) custom-call(f32[4]{0:T(128)} %ext_hbm.1, s32[512]{0:T(512)} %bitcast.2, f32[16,32,512]{2,1,0:T(8,128)} %control_ref.1, ...), custom_call_target="tpu_custom_call" | custom-call | tf_op jit(solution)/shard_map/pallas_call | solution.py:727
  39.1 0.0 copy-start.5
  39.1 0.0 copy-start.6
  39.1 0.0 copy-done
  39.1 0.0 copy-done.4
  39.2 0.0 copy-done.10
  39.2 0.0 copy-start.7
  39.2 1.0 %copy-done.7 = bf16[512,128]{1,0:T(8,128)(2,1)S(1)} copy-done((bf16[512,128]{1,0:T(8,128)(2,1)S(1)}, bf16[512,128]{1,0:T(8,128)(2,1)}, u32[]{:S(2)}) %copy-start.7) | copy-done | bytes 131096
  40.2 0.0 copy-start.8
  40.2 0.0 copy-start.9
  40.2 6.1 %shard_map.119.x_ref = bf16[8,80,128]{2,1,0:T(8,128)(2,1)S(1)} custom-call(s32[512]{0:T(512)S(1)} %bitcast.3, bf16[512,16,128]{2,1,0:T(8,128)(2,1)S(1)} %copy-done, s32[512,128]{1,0:T(8,128)S(1)} %copy-done.4, bf16[512,128]{1,0:T(8,128)(2,1)S(1)} %copy-done.7), custom_call_target="tpu_custom_call" | custom-call | tf_op jit(solution)/shard_map/pallas_call | solution.py:799
  46.2 0.0 copy-done.5
  46.2 0.0 copy-done.6
  46.3 0.0 copy-done.8
  46.3 0.0 copy-done.9
  46.3 0.0 copy-start.1
  46.3 0.0 copy-start.2
  46.3 0.0 copy-start.3
  46.3 11.3 %shard_map.120.levels_ref = f32[2,256,640]{2,1,0:T(8,128)S(1)} custom-call(bf16[8,80,128]{2,1,0:T(8,128)(2,1)S(1)} %shard_map.119.x_ref, bf16[1,64,16,512]{3,2,1,0:T(8,128)(2,1)S(1)} %copy-done.5, bf16[4,8,16,512]{3,2,1,0:T(8,128)(2,1)S(1)} %copy-done.6, bf16[8,16,512]{2,1,0:T(8,128)(2,1)S(1)} %copy-done.8, bf16[4,2,16,128]{3,2,1,0:T(8,128)(2,1)S(1)} %copy-done.9, ...), custom_call_target="tpu_custom_call" | custom-call | tf_op jit(solution)/shard_map/pallas_call | solution.py:808
  57.7 0.0 copy-done.1
  57.7 0.0 copy-done.2
  57.7 0.0 copy-done.3
  57.7 2.2 %shard_map.121 = f32[16,32,512]{2,1,0:T(8,128)} custom-call(f32[2,256,640]{2,1,0:T(8,128)S(1)} %shard_map.120.levels_ref, bf16[640,512]{1,0:T(8,128)(2,1)S(1)} %copy-done.3, bf16[640,512]{1,0:T(8,128)(2,1)S(1)} %copy-done.2, f32[16,32,512]{2,1,0:T(8,128)S(1)} %copy-done.1), custom_call_target="tpu_custom_call" | custom-call | tf_op jit(solution)/shard_map/pallas_call | solution.py:831
Async XLA Ops:
  0.0 39.1 %copy-start = (bf16[512,16,128]{2,1,0:T(8,128)(2,1)S(1)}, bf16[512,16,128]{2,1,0:T(8,128)(2,1)}, u32[]{:S(2)}) copy-start(bf16[512,16,128]{2,1,0:T(8,128)(2,1)} %kern_ref.1) | copy-start | bytes 6291460
  0.0 39.1 %copy-start.4 = (s32[512,128]{1,0:T(8,128)S(1)}, s32[512,128]{1,0:T(8,128)}, u32[]{:S(2)}) copy-start(s32[512,128]{1,0:T(8,128)} %col_ref.1) | copy-start | bytes 786436
  0.0 39.1 %copy-start.10 = (s32[512,1]{0,1:T(1,128)S(1)}, s32[512,1]{0,1:T(1,128)}, u32[]{:S(2)}) copy-start(s32[512,1]{0,1:T(1,128)} %param.18) | copy-start | bytes 6148
  39.1 7.1 %copy-start.5 = (bf16[1,64,16,512]{3,2,1,0:T(8,128)(2,1)S(1)}, bf16[1,64,16,512]{3,2,1,0:T(8,128)(2,1)}, u32[]{:S(2)}) copy-start(bf16[1,64,16,512]{3,2,1,0:T(8,128)(2,1)} %get-tuple-element.11.mixed_hbm) | copy-start | bytes 3145732
  39.1 7.1 %copy-start.6 = (bf16[4,8,16,512]{3,2,1,0:T(8,128)(2,1)S(1)}, bf16[4,8,16,512]{3,2,1,0:T(8,128)(2,1)}, u32[]{:S(2)}) copy-start(bf16[4,8,16,512]{3,2,1,0:T(8,128)(2,1)} %get-tuple-element.12.low_hbm) | copy-start | bytes 1572868
  39.2 1.0 %copy-start.7 = (bf16[512,128]{1,0:T(8,128)(2,1)S(1)}, bf16[512,128]{1,0:T(8,128)(2,1)}, u32[]{:S(2)}) copy-start(bf16[512,128]{1,0:T(8,128)(2,1)} %get-tuple-element.10.mis_ref) | copy-start | bytes 393220
  40.2 6.1 %copy-start.8 = (bf16[8,16,512]{2,1,0:T(8,128)(2,1)S(1)}, bf16[8,16,512]{2,1,0:T(8,128)(2,1)}, u32[]{:S(2)}) copy-start(bf16[8,16,512]{2,1,0:T(8,128)(2,1)} %get-tuple-element.13.rest_hbm) | copy-start | bytes 393220
  40.2 6.1 %copy-start.9 = (bf16[4,2,16,128]{3,2,1,0:T(8,128)(2,1)S(1)}, bf16[4,2,16,128]{3,2,1,0:T(8,128)(2,1)}, u32[]{:S(2)}) copy-start(bf16[4,2,16,128]{3,2,1,0:T(8,128)(2,1)} %get-tuple-element.14.edge_hbm) | copy-start | bytes 98308
  46.3 11.4 %copy-start.1 = (f32[16,32,512]{2,1,0:T(8,128)S(1)}, f32[16,32,512]{2,1,0:T(8,128)}, u32[]{:S(2)}) copy-start(f32[16,32,512]{2,1,0:T(8,128)} %control_ref.1) | copy-start | bytes 3145732
  46.3 11.4 %copy-start.2 = (bf16[640,512]{1,0:T(8,128)(2,1)S(1)}, bf16[640,512]{1,0:T(8,128)(2,1)}, u32[]{:S(2)}) copy-start(bf16[640,512]{1,0:T(8,128)(2,1)} %constant.8.clone.lo_hbm.lo_ref) | copy-start | bytes 1966084
  46.3 11.4 %copy-start.3 = (bf16[640,512]{1,0:T(8,128)(2,1)S(1)}, bf16[640,512]{1,0:T(8,128)(2,1)}, u32[]{:S(2)}) copy-start(bf16[640,512]{1,0:T(8,128)(2,1)} %constant.7.clone.hi_hbm.hi_ref) | copy-start | bytes 1966084
